TPU v7x, 32 devices: a whole 2x2x4 slice. The times are simulated.
32 devices in a mesh: farm: 2 (over x), blk: 16 (over z, y, core).
Axes of the slice: x: 2, y: 2, z: 4, core: 2. Of those that a mesh axis runs over, the one named last changes fastest.
Arguments:
- particle_pos: float32 [3, 65536], P(None, ('farm', 'blk')), parts along dimension 1, may hold values from -2 to 2
- vorticity: float32 [3, 65536], P(None, ('farm', 'blk')), parts along dimension 1, may hold values from -6 to 6
- particle_owner: int32 [65536], P(('farm', 'blk')), parts along dimension 0, may hold values from 0 to 15, as said below
- thrust_coef: float32 [32], P('farm'), parts along dimension 0, may hold values from 0.3 to 1
- node_pos: float32 [3, 4096], P(None, ('farm', 'blk')), parts along dimension 1, may hold values from -2 to 2
- lever_arm: float32 [3, 4096], P(None, ('farm', 'blk')), parts along dimension 1, may hold values from -1 to 1
- chord_coef: float32 [4096], P(('farm', 'blk')), parts along dimension 0, may hold values from 0.005 to 0.02
- node_platform: int32 [4096], P(('farm', 'blk')), parts along dimension 0, may hold values from 0 to 15, as said below
- platform_pos: float32 [6, 32], P(None, ('farm', 'blk')), parts along dimension 1, may hold values from -0.3 to 0.3
- platform_vel: float32 [6, 32], P(None, ('farm', 'blk')), parts along dimension 1, may hold values from -1.5 to 1.5
- velocity_history: float32 [32, 6, 1024], P(('farm', 'blk')), parts along dimension 0, may hold values from -6 to 6
- memory_kernel: float32 [6, 6, 1024], replicated, may hold values from -0.078125 to 0.078125
- restoring: float32 [6], replicated, may hold values from 1 to 4
- inverse_mass: float32 [6, 6], replicated, may hold values from -0.15 to 1, as said below
- line_offset: float32 [3, 96, 128], P(None, ('farm', 'blk')), parts along dimension 1, may hold values from -0.3125 to 0.3125
- line_velocity: float32 [3, 96, 128], P(None, ('farm', 'blk')), parts along dimension 1, may hold values from -6 to 6
- line_platform: int32 [96], P(('farm', 'blk')), parts along dimension 0, may hold values from 0 to 15, as said below
Outputs:
- induced_velocity: float32 [3, 65536], P(None, ('farm', 'blk')), parts along dimension 1
- platform_accel: float32 [6, 32], P(None, ('farm', 'blk')), parts along dimension 1
- line_accel: float32 [3, 96, 128], P(None, ('farm', 'blk')), parts along dimension 1
There are 2 independent parts, one for each index of `farm`. A program takes and returns all parts, laid end to end along the dimension named above; an argument that names none is the same for every part. Nothing has to cross between parts.
Inputs may be any that keep to these rules, and one draw needn't show every extreme that they name: `particle_owner`: each turbine shed exactly 2048 particles. `node_platform`: each platform carries exactly 128 nodes. `line_platform`: each platform holds exactly 3 lines. `inverse_mass`: diagonal between 0.5 and 1, other entries between -0.15 and 0.15.
All inputs are finite; a program needn't handle non-finite values.
Results may differ from a plain program's by a relative error of at most 0.0003.
Values sent between devices are 32-bit elements; how exact they have to be, the bound alone decides.
No kernel may reach another device: no remote copies, remote signals or barrier semaphores. Data moves between devices by JAX's collectives and lax.ppermute only.
A program may use at most 64 MiB of HBM per device.

v0:
```python
import math

import jax
import jax.numpy as jnp
from jax import lax
from jax.sharding import PartitionSpec as P

core_square = 0.01
inverse_four_pi = 0.25 / math.pi
line_spacing = 1.0
rest_length = 0.95 * math.sqrt(1.36)
line_stiffness = 20.0
node_weight = 0.5
line_damping = 0.5
high_precision = lax.Precision.HIGHEST


def cross_product(first, second):
    return jnp.stack(
        [
            first[1] * second[2] - first[2] * second[1],
            first[2] * second[0] - first[0] * second[2],
            first[0] * second[1] - first[1] * second[0],
        ]
    )


def induced(targets, sources, strengths, block_len):
    blocks_in = sources.shape[1] // block_len
    source_blocks = sources.reshape(3, blocks_in, block_len).transpose(1, 0, 2)
    strength_blocks = strengths.reshape(3, blocks_in, block_len).transpose(1, 0, 2)

    def advance(running, block_pair):
        where_from, circulation = block_pair
        sep_x = targets[0][:, None] - where_from[0][None, :]
        sep_y = targets[1][:, None] - where_from[1][None, :]
        sep_z = targets[2][:, None] - where_from[2][None, :]
        dist_sq = sep_x * sep_x + sep_y * sep_y + sep_z * sep_z + core_square
        kernel_value = lax.rsqrt(dist_sq) / dist_sq * inverse_four_pi
        vel_x = jnp.sum(
            kernel_value * (circulation[1][None, :] * sep_z - circulation[2][None, :] * sep_y),
            axis=1,
        )
        vel_y = jnp.sum(
            kernel_value * (circulation[2][None, :] * sep_x - circulation[0][None, :] * sep_z),
            axis=1,
        )
        vel_z = jnp.sum(
            kernel_value * (circulation[0][None, :] * sep_y - circulation[1][None, :] * sep_x),
            axis=1,
        )
        return (running + jnp.stack([vel_x, vel_y, vel_z]), None)

    running, unused = lax.scan(
        advance, jnp.zeros(targets.shape, jnp.float32), (source_blocks, strength_blocks)
    )
    return running


def blade_terms(node_induced, node_motion, lever_arm, chord_coef):
    rigid = node_motion[:3] + cross_product(node_motion[3:], lever_arm)
    stream = jnp.array([1.0, 0.0, 0.0], jnp.float32)[:, None]
    relative = stream + node_induced - rigid
    magnitude = jnp.sqrt(jnp.sum(relative * relative, axis=0))
    node_force = (chord_coef * magnitude)[None, :] * relative
    return jnp.concatenate([node_force, cross_product(lever_arm, node_force)], axis=0)


def mooring(line_offset, line_velocity, line_index, fairlead):
    bearing = 2.0 * math.pi / 3.0 * (line_index % 3).astype(jnp.float32)
    heading = jnp.stack(
        [jnp.cos(bearing), jnp.sin(bearing), jnp.full(bearing.shape, 0.6, jnp.float32)]
    )
    segments_total = line_offset.shape[2]
    depth_steps = (segments_total - jnp.arange(segments_total)).astype(jnp.float32)
    positions = -line_spacing * heading[:, :, None] * depth_steps[None, None, :] + line_offset
    following = jnp.concatenate([positions[:, :, 1:], fairlead[:, :, None]], axis=2)
    segment = following - positions
    lengths = jnp.sqrt(jnp.sum(segment * segment, axis=0))
    tension = line_stiffness * (lengths - rest_length) / rest_length
    pull = (tension / lengths)[None] * segment
    previous = jnp.concatenate([jnp.zeros_like(pull[:, :, :1]), pull[:, :, :-1]], axis=2)
    gravity = jnp.array([0.0, 0.0, -node_weight], jnp.float32)[:, None, None]
    node_force = pull - previous + gravity - line_damping * line_velocity
    movable = (jnp.arange(segments_total) > 0).astype(jnp.float32)
    return (node_force * movable[None, None, :], -pull[:, :, -1])


def shards(
    particle_pos,
    vorticity,
    particle_owner,
    thrust_coef,
    node_pos,
    lever_arm,
    chord_coef,
    node_platform,
    platform_pos,
    platform_vel,
    velocity_history,
    memory_kernel,
    restoring,
    inverse_mass,
    line_offset,
    line_velocity,
    line_platform,
):
    every_pos, every_vel = (
        lax.all_gather(platform_pos, "blk", axis=1, tiled=True),
        lax.all_gather(platform_vel, "blk", axis=1, tiled=True),
    )
    platforms = every_pos.shape[1]
    columns = jnp.arange(platforms, dtype=jnp.int32)
    owner_hot = (particle_owner[:, None] == columns[None, :]).astype(jnp.float32)
    owner_thrust = jnp.dot(owner_hot, thrust_coef, precision=high_precision)
    owner_surge = jnp.dot(owner_hot, every_vel[0], precision=high_precision)
    strengths = vorticity * (owner_thrust * (1.0 - owner_surge))[None, :]
    node_hot = (node_platform[:, None] == columns[None, :]).astype(jnp.float32)
    node_shift = jnp.dot(every_pos, node_hot.T, precision=high_precision)
    node_motion = jnp.dot(every_vel, node_hot.T, precision=high_precision)
    current = node_pos + node_shift[:3]
    own_count = particle_pos.shape[1]
    targets = jnp.concatenate([particle_pos, current], axis=1)
    velocity = induced(
        targets,
        lax.all_gather(particle_pos, "blk", axis=1, tiled=True),
        lax.all_gather(strengths, "blk", axis=1, tiled=True),
        own_count,
    )
    induced_velocity = velocity[:, :own_count]
    node_terms = blade_terms(velocity[:, own_count:], node_motion, lever_arm, chord_coef)
    line_count = line_offset.shape[1]
    line_index = lax.axis_index("blk") * line_count + jnp.arange(line_count, dtype=jnp.int32)
    line_hot = (line_platform[:, None] == columns[None, :]).astype(jnp.float32)
    fairlead = jnp.dot(every_pos[:3], line_hot.T, precision=high_precision)
    line_accel, fairlead_pull = mooring(line_offset, line_velocity, line_index, fairlead)
    line_terms = jnp.concatenate([fairlead_pull, jnp.zeros_like(fairlead_pull)], axis=0)
    platform_terms = jnp.dot(node_terms, node_hot, precision=high_precision)
    platform_terms = platform_terms + jnp.dot(line_terms, line_hot, precision=high_precision)
    loads = lax.psum_scatter(platform_terms, "blk", scatter_dimension=1, tiled=True)
    radiation = -jnp.einsum(
        "ijk,pjk->ip", memory_kernel, velocity_history, precision=high_precision
    )
    total = loads + radiation - restoring[:, None] * platform_pos
    platform_accel = jnp.dot(inverse_mass, total, precision=high_precision)
    return (induced_velocity, platform_accel, line_accel)


def solution(mesh):
    return jax.shard_map(
        shards,
        mesh=mesh,
        in_specs=(
            P(None, ("farm", "blk")),
            P(None, ("farm", "blk")),
            P(("farm", "blk")),
            P("farm"),
            P(None, ("farm", "blk")),
            P(None, ("farm", "blk")),
            P(("farm", "blk")),
            P(("farm", "blk")),
            P(None, ("farm", "blk")),
            P(None, ("farm", "blk")),
            P(("farm", "blk"), None, None),
            P(),
            P(),
            P(),
            P(None, ("farm", "blk"), None),
            P(None, ("farm", "blk"), None),
            P(("farm", "blk")),
        ),
        out_specs=(
            P(None, ("farm", "blk")),
            P(None, ("farm", "blk")),
            P(None, ("farm", "blk"), None),
        ),
        check_vma=False,
    )
```

profile of v0, /device:TPU:0, one launch (start us, length us, event | category | flops | bytes accessed | tf_op | source)
XLA Modules:
  0.0 509.8 jit_solution(4682129688845925740)
XLA Ops:
  0.7 23.2 %all-gather.1 = f32[16,1,6]{2,1,0:T(1,128)S(1)} all-gather(f32[1,1,6]{2,1,0:T(1,128)} %bitcast.101), channel_id=1, replica_groups=mesh['farm'=2,'blk'=16] {'blk'}, dimensions={0}, use_global_device_ids=true | all-gather | bytes 408 | tf_op jit(solution)/shard_map/all_gather | solution.py:110
  23.8 0.8 convolution_bitcast_fusion
  24.7 0.9 multiply_subtract_fusion.5
  25.5 0.1 copy.35
  25.6 1.4 fusion.17
  27.1 1.4 fusion.18
  28.6 18.8 %all_gather.15 = f32[3,32768]{1,0:T(4,128)S(1)} all-gather(f32[3,2048]{1,0:T(4,128)S(1)} %broadcast_multiply_fusion), channel_id=1, replica_groups=mesh['farm'=2,'blk'=16] {'blk'}, dimensions={1}, use_global_device_ids=true | all-gather | bytes 417792 | tf_op jit(solution)/shard_map/all_gather | solution.py:127
  47.4 18.7 %all-gather = f32[16,1,6]{2,1,0:T(1,128)S(1)} all-gather(f32[1,1,6]{2,1,0:T(1,128)S(1)} %bitcast.100), channel_id=1, replica_groups=mesh['farm'=2,'blk'=16] {'blk'}, dimensions={0}, use_global_device_ids=true | all-gather | bytes 408 | tf_op jit(solution)/shard_map/all_gather | solution.py:109
  66.1 0.2 convolution_bitcast_fusion.1
  66.4 18.8 %all_gather.13 = f32[3,32768]{1,0:T(4,128)S(1)} all-gather(f32[3,2048]{1,0:T(4,128)S(1)} %copy-done.2), channel_id=1, replica_groups=mesh['farm'=2,'blk'=16] {'blk'}, dimensions={1}, use_global_device_ids=true | all-gather | bytes 417792 | tf_op jit(solution)/shard_map/all_gather | solution.py:126
  85.3 387.2 %while.11 = (s32[]{:T(128)}, f32[3,2176]{1,0:T(4,128)S(1)}, f32[3,2176]{1,0:T(4,128)S(1)}, f32[16,3,2048]{2,1,0:T(4,128)S(1)}, f32[16,3,2048]{2,1,0:T(4,128)S(1)}, /*index=5*/s32[]{:T(128)}, s32[]{:T(128)}, s32[]{}, s32[]{}) while((s32[]{:T(128)}, f32[3,2176]{1,0:T(4,128)S(1)}, f32[3,2176]{1,0:T(4,128)S(1)}, ...), condition=%wide.region_4.5_spmd.clone, body=%wide.region_0.4_spmd.clone.sunk | while | flops 115887232 | bytes 382603 | solution.py:54
  85.4 0.1 slice_reduce_fusion.4
  85.5 23.9 %fusion.55 = (f32[2176]{0:T(1024)S(1)}, f32[2176]{0:T(1024)S(1)}, f32[2176]{0:T(1024)S(1)}) fusion(f32[2048]{0:T(1024)S(1)} %bitcast.91, f32[2048]{0:T(1024)S(1)} %bitcast.90, f32[2048]{0:T(1024)S(1)} %bitcast.89, f32[2176]{0:T(1024)S(1)} %get-tuple-element.130, f32[2048]{0:T(1024)S(1)} %bitcast.88, f32[2176]{0:T(1024)S(1)} %get-tuple-element.132, ...), kind=kLoop, calls=%fused_computation.22.clone.1 | loop fusion | flops 115861120 | bytes 101376 | tf_op jit(solution)/shard_map/while/body/eval_jaxpr/reduce_sum | solution.py:40
  109.5 0.1 maximum_add_fusion.3
  109.6 0.1 slice_reduce_fusion.4
  109.7 23.9 %fusion.55 = (f32[2176]{0:T(1024)S(1)}, f32[2176]{0:T(1024)S(1)}, f32[2176]{0:T(1024)S(1)}) fusion(f32[2048]{0:T(1024)S(1)} %bitcast.91, f32[2048]{0:T(1024)S(1)} %bitcast.90, f32[2048]{0:T(1024)S(1)} %bitcast.89, f32[2176]{0:T(1024)S(1)} %get-tuple-element.130, f32[2048]{0:T(1024)S(1)} %bitcast.88, f32[2176]{0:T(1024)S(1)} %get-tuple-element.132, ...), kind=kLoop, calls=%fused_computation.22.clone.1 | loop fusion | flops 115861120 | bytes 101376 | tf_op jit(solution)/shard_map/while/body/eval_jaxpr/reduce_sum | solution.py:40
  133.8 0.1 slice_reduce_fusion.4
  133.8 23.9 %fusion.55 = (f32[2176]{0:T(1024)S(1)}, f32[2176]{0:T(1024)S(1)}, f32[2176]{0:T(1024)S(1)}) fusion(f32[2048]{0:T(1024)S(1)} %bitcast.91, f32[2048]{0:T(1024)S(1)} %bitcast.90, f32[2048]{0:T(1024)S(1)} %bitcast.89, f32[2176]{0:T(1024)S(1)} %get-tuple-element.130, f32[2048]{0:T(1024)S(1)} %bitcast.88, f32[2176]{0:T(1024)S(1)} %get-tuple-element.132, ...), kind=kLoop, calls=%fused_computation.22.clone.1 | loop fusion | flops 115861120 | bytes 101376 | tf_op jit(solution)/shard_map/while/body/eval_jaxpr/reduce_sum | solution.py:40
  158.0 0.1 slice_reduce_fusion.4
  158.0 23.9 %fusion.55 = (f32[2176]{0:T(1024)S(1)}, f32[2176]{0:T(1024)S(1)}, f32[2176]{0:T(1024)S(1)}) fusion(f32[2048]{0:T(1024)S(1)} %bitcast.91, f32[2048]{0:T(1024)S(1)} %bitcast.90, f32[2048]{0:T(1024)S(1)} %bitcast.89, f32[2176]{0:T(1024)S(1)} %get-tuple-element.130, f32[2048]{0:T(1024)S(1)} %bitcast.88, f32[2176]{0:T(1024)S(1)} %get-tuple-element.132, ...), kind=kLoop, calls=%fused_computation.22.clone.1 | loop fusion | flops 115861120 | bytes 101376 | tf_op jit(solution)/shard_map/while/body/eval_jaxpr/reduce_sum | solution.py:40
  182.2 0.1 slice_reduce_fusion.4
  182.2 23.9 %fusion.55 = (f32[2176]{0:T(1024)S(1)}, f32[2176]{0:T(1024)S(1)}, f32[2176]{0:T(1024)S(1)}) fusion(f32[2048]{0:T(1024)S(1)} %bitcast.91, f32[2048]{0:T(1024)S(1)} %bitcast.90, f32[2048]{0:T(1024)S(1)} %bitcast.89, f32[2176]{0:T(1024)S(1)} %get-tuple-element.130, f32[2048]{0:T(1024)S(1)} %bitcast.88, f32[2176]{0:T(1024)S(1)} %get-tuple-element.132, ...), kind=kLoop, calls=%fused_computation.22.clone.1 | loop fusion | flops 115861120 | bytes 101376 | tf_op jit(solution)/shard_map/while/body/eval_jaxpr/reduce_sum | solution.py:40
  206.4 0.1 slice_reduce_fusion.4
  206.4 23.9 %fusion.55 = (f32[2176]{0:T(1024)S(1)}, f32[2176]{0:T(1024)S(1)}, f32[2176]{0:T(1024)S(1)}) fusion(f32[2048]{0:T(1024)S(1)} %bitcast.91, f32[2048]{0:T(1024)S(1)} %bitcast.90, f32[2048]{0:T(1024)S(1)} %bitcast.89, f32[2176]{0:T(1024)S(1)} %get-tuple-element.130, f32[2048]{0:T(1024)S(1)} %bitcast.88, f32[2176]{0:T(1024)S(1)} %get-tuple-element.132, ...), kind=kLoop, calls=%fused_computation.22.clone.1 | loop fusion | flops 115861120 | bytes 101376 | tf_op jit(solution)/shard_map/while/body/eval_jaxpr/reduce_sum | solution.py:40
  230.6 0.1 slice_reduce_fusion.4
  230.6 23.9 %fusion.55 = (f32[2176]{0:T(1024)S(1)}, f32[2176]{0:T(1024)S(1)}, f32[2176]{0:T(1024)S(1)}) fusion(f32[2048]{0:T(1024)S(1)} %bitcast.91, f32[2048]{0:T(1024)S(1)} %bitcast.90, f32[2048]{0:T(1024)S(1)} %bitcast.89, f32[2176]{0:T(1024)S(1)} %get-tuple-element.130, f32[2048]{0:T(1024)S(1)} %bitcast.88, f32[2176]{0:T(1024)S(1)} %get-tuple-element.132, ...), kind=kLoop, calls=%fused_computation.22.clone.1 | loop fusion | flops 115861120 | bytes 101376 | tf_op jit(solution)/shard_map/while/body/eval_jaxpr/reduce_sum | solution.py:40
  254.8 0.1 slice_reduce_fusion.4
  254.8 23.9 %fusion.55 = (f32[2176]{0:T(1024)S(1)}, f32[2176]{0:T(1024)S(1)}, f32[2176]{0:T(1024)S(1)}) fusion(f32[2048]{0:T(1024)S(1)} %bitcast.91, f32[2048]{0:T(1024)S(1)} %bitcast.90, f32[2048]{0:T(1024)S(1)} %bitcast.89, f32[2176]{0:T(1024)S(1)} %get-tuple-element.130, f32[2048]{0:T(1024)S(1)} %bitcast.88, f32[2176]{0:T(1024)S(1)} %get-tuple-element.132, ...), kind=kLoop, calls=%fused_computation.22.clone.1 | loop fusion | flops 115861120 | bytes 101376 | tf_op jit(solution)/shard_map/while/body/eval_jaxpr/reduce_sum | solution.py:40
  279.0 0.1 slice_reduce_fusion.4
  279.0 23.9 %fusion.55 = (f32[2176]{0:T(1024)S(1)}, f32[2176]{0:T(1024)S(1)}, f32[2176]{0:T(1024)S(1)}) fusion(f32[2048]{0:T(1024)S(1)} %bitcast.91, f32[2048]{0:T(1024)S(1)} %bitcast.90, f32[2048]{0:T(1024)S(1)} %bitcast.89, f32[2176]{0:T(1024)S(1)} %get-tuple-element.130, f32[2048]{0:T(1024)S(1)} %bitcast.88, f32[2176]{0:T(1024)S(1)} %get-tuple-element.132, ...), kind=kLoop, calls=%fused_computation.22.clone.1 | loop fusion | flops 115861120 | bytes 101376 | tf_op jit(solution)/shard_map/while/body/eval_jaxpr/reduce_sum | solution.py:40
  303.2 0.1 slice_reduce_fusion.4
  303.2 23.9 %fusion.55 = (f32[2176]{0:T(1024)S(1)}, f32[2176]{0:T(1024)S(1)}, f32[2176]{0:T(1024)S(1)}) fusion(f32[2048]{0:T(1024)S(1)} %bitcast.91, f32[2048]{0:T(1024)S(1)} %bitcast.90, f32[2048]{0:T(1024)S(1)} %bitcast.89, f32[2176]{0:T(1024)S(1)} %get-tuple-element.130, f32[2048]{0:T(1024)S(1)} %bitcast.88, f32[2176]{0:T(1024)S(1)} %get-tuple-element.132, ...), kind=kLoop, calls=%fused_computation.22.clone.1 | loop fusion | flops 115861120 | bytes 101376 | tf_op jit(solution)/shard_map/while/body/eval_jaxpr/reduce_sum | solution.py:40
  327.4 0.1 slice_reduce_fusion.4
  327.4 23.9 %fusion.55 = (f32[2176]{0:T(1024)S(1)}, f32[2176]{0:T(1024)S(1)}, f32[2176]{0:T(1024)S(1)}) fusion(f32[2048]{0:T(1024)S(1)} %bitcast.91, f32[2048]{0:T(1024)S(1)} %bitcast.90, f32[2048]{0:T(1024)S(1)} %bitcast.89, f32[2176]{0:T(1024)S(1)} %get-tuple-element.130, f32[2048]{0:T(1024)S(1)} %bitcast.88, f32[2176]{0:T(1024)S(1)} %get-tuple-element.132, ...), kind=kLoop, calls=%fused_computation.22.clone.1 | loop fusion | flops 115861120 | bytes 101376 | tf_op jit(solution)/shard_map/while/body/eval_jaxpr/reduce_sum | solution.py:40
  351.6 0.1 slice_reduce_fusion.4
  351.6 23.9 %fusion.55 = (f32[2176]{0:T(1024)S(1)}, f32[2176]{0:T(1024)S(1)}, f32[2176]{0:T(1024)S(1)}) fusion(f32[2048]{0:T(1024)S(1)} %bitcast.91, f32[2048]{0:T(1024)S(1)} %bitcast.90, f32[2048]{0:T(1024)S(1)} %bitcast.89, f32[2176]{0:T(1024)S(1)} %get-tuple-element.130, f32[2048]{0:T(1024)S(1)} %bitcast.88, f32[2176]{0:T(1024)S(1)} %get-tuple-element.132, ...), kind=kLoop, calls=%fused_computation.22.clone.1 | loop fusion | flops 115861120 | bytes 101376 | tf_op jit(solution)/shard_map/while/body/eval_jaxpr/reduce_sum | solution.py:40
  375.8 0.1 slice_reduce_fusion.4
  375.8 23.9 %fusion.55 = (f32[2176]{0:T(1024)S(1)}, f32[2176]{0:T(1024)S(1)}, f32[2176]{0:T(1024)S(1)}) fusion(f32[2048]{0:T(1024)S(1)} %bitcast.91, f32[2048]{0:T(1024)S(1)} %bitcast.90, f32[2048]{0:T(1024)S(1)} %bitcast.89, f32[2176]{0:T(1024)S(1)} %get-tuple-element.130, f32[2048]{0:T(1024)S(1)} %bitcast.88, f32[2176]{0:T(1024)S(1)} %get-tuple-element.132, ...), kind=kLoop, calls=%fused_computation.22.clone.1 | loop fusion | flops 115861120 | bytes 101376 | tf_op jit(solution)/shard_map/while/body/eval_jaxpr/reduce_sum | solution.py:40
  400.0 0.1 slice_reduce_fusion.4
  400.0 23.9 %fusion.55 = (f32[2176]{0:T(1024)S(1)}, f32[2176]{0:T(1024)S(1)}, f32[2176]{0:T(1024)S(1)}) fusion(f32[2048]{0:T(1024)S(1)} %bitcast.91, f32[2048]{0:T(1024)S(1)} %bitcast.90, f32[2048]{0:T(1024)S(1)} %bitcast.89, f32[2176]{0:T(1024)S(1)} %get-tuple-element.130, f32[2048]{0:T(1024)S(1)} %bitcast.88, f32[2176]{0:T(1024)S(1)} %get-tuple-element.132, ...), kind=kLoop, calls=%fused_computation.22.clone.1 | loop fusion | flops 115861120 | bytes 101376 | tf_op jit(solution)/shard_map/while/body/eval_jaxpr/reduce_sum | solution.py:40
  424.2 0.1 slice_reduce_fusion.4
  424.2 23.9 %fusion.55 = (f32[2176]{0:T(1024)S(1)}, f32[2176]{0:T(1024)S(1)}, f32[2176]{0:T(1024)S(1)}) fusion(f32[2048]{0:T(1024)S(1)} %bitcast.91, f32[2048]{0:T(1024)S(1)} %bitcast.90, f32[2048]{0:T(1024)S(1)} %bitcast.89, f32[2176]{0:T(1024)S(1)} %get-tuple-element.130, f32[2048]{0:T(1024)S(1)} %bitcast.88, f32[2176]{0:T(1024)S(1)} %get-tuple-element.132, ...), kind=kLoop, calls=%fused_computation.22.clone.1 | loop fusion | flops 115861120 | bytes 101376 | tf_op jit(solution)/shard_map/while/body/eval_jaxpr/reduce_sum | solution.py:40
  448.4 0.1 slice_reduce_fusion.4
  448.4 23.9 %fusion.55 = (f32[2176]{0:T(1024)S(1)}, f32[2176]{0:T(1024)S(1)}, f32[2176]{0:T(1024)S(1)}) fusion(f32[2048]{0:T(1024)S(1)} %bitcast.91, f32[2048]{0:T(1024)S(1)} %bitcast.90, f32[2048]{0:T(1024)S(1)} %bitcast.89, f32[2176]{0:T(1024)S(1)} %get-tuple-element.130, f32[2048]{0:T(1024)S(1)} %bitcast.88, f32[2176]{0:T(1024)S(1)} %get-tuple-element.132, ...), kind=kLoop, calls=%fused_computation.22.clone.1 | loop fusion | flops 115861120 | bytes 101376 | tf_op jit(solution)/shard_map/while/body/eval_jaxpr/reduce_sum | solution.py:40
  472.5 0.1 multiply_reduce_fusion.1
  472.7 0.3 fusion.22
  472.9 0.1 fusion.45
  473.0 0.1 pad.9.clone
  473.1 0.1 maximum_multiply_fusion
  473.2 0.1 multiply_add_fusion
  473.2 0.1 slice.136
  473.3 0.1 copy.34
  473.4 0.2 convolution_bitcast_fusion.2
  473.6 0.1 copy.37
  473.7 0.1 multiply_reduce_fusion
  473.8 0.1 broadcast_multiply_fusion.1
  473.9 0.2 fusion.27
  474.1 0.3 convolution_add_fusion
  474.3 31.7 %all-reduce.2 = f32[6,16]{0,1:T(8,128)S(1)} all-reduce(f32[6,16]{0,1:T(8,128)S(1)} %convolution_add_fusion), channel_id=2, replica_groups=mesh['farm'=2,'blk'=16] {'blk'}, use_global_device_ids=true, to_apply=%region_7.8.clone | all-reduce | flops 96 | bytes 768
  506.0 0.6 dynamic-slice
  506.6 1.2 fusion.16
  507.8 0.7 convolution_bitcast_fusion.3
  508.5 0.7 subtract_multiply_fusion.10
  509.2 0.6 slice.111
  (124 shorter events, 2.2 us)
Async XLA Ops:
  0.6 506.0 %copy-start = (f32[1,6,1024]{2,0,1:T(1,128)S(1)}, f32[1,6,1024]{2,0,1:T(1,128)}, u32[]{:S(2)}) copy-start(f32[1,6,1024]{2,0,1:T(1,128)} %param.31) | copy-start | bytes 73732
  0.6 27.9 %copy-start.4 = (f32[3,2048]{1,0:T(4,128)S(1)}, f32[3,2048]{1,0:T(4,128)}, u32[]{:S(2)}) copy-start(f32[3,2048]{1,0:T(4,128)} %param.22) | copy-start | bytes 73732
  27.0 20.4 %copy-start.8 = (f32[6,1]{0,1:T(1,128)S(1)}, f32[6,1]{0,1:T(1,128)}, u32[]{:S(2)}) copy-start(f32[6,1]{0,1:T(1,128)} %param.29) | copy-start | bytes 76
  27.0 39.1 %copy-start.14 = (s32[128]{0:T(128)S(1)}, s32[128]{0:T(128)}, u32[]{:S(2)}) copy-start(s32[128]{0:T(128)} %param.28) | copy-start | bytes 1540
  27.0 39.3 %copy-start.9 = (f32[3,128]{1,0:T(4,128)S(1)}, f32[3,128]{1,0:T(4,128)}, u32[]{:S(2)}) copy-start(f32[3,128]{1,0:T(4,128)} %param.25) | copy-start | bytes 4612
  27.0 39.3 %copy-start.2 = (f32[3,2048]{1,0:T(4,128)S(1)}, f32[3,2048]{1,0:T(4,128)}, u32[]{:S(2)}) copy-start(f32[3,2048]{1,0:T(4,128)} %param.21) | copy-start | bytes 73732
  85.2 387.3 %copy-start.12 = (f32[3]{0:T(128)S(1)}, f32[3]{0:T(128)}, u32[]{:S(2)}) copy-start(f32[3]{0:T(128)} %constant.60.clone) | copy-start | bytes 40
  85.2 387.4 %copy-start.13 = (f32[128]{0:T(128)S(1)}, f32[128]{0:T(128)}, u32[]{:S(2)}) copy-start(f32[128]{0:T(128)} %param.27) | copy-start | bytes 1540
  85.2 387.4 %copy-start.6 = (f32[3,128]{1,0:T(4,128)S(1)}, f32[3,128]{1,0:T(4,128)}, u32[]{:S(2)}) copy-start(f32[3,128]{1,0:T(4,128)} %param.26) | copy-start | bytes 4612
  85.2 387.9 %copy-start.3 = (f32[3,3,128]{2,1,0:T(4,128)S(1)}, f32[3,3,128]{2,1,0:T(4,128)}, u32[]{:S(2)}) copy-start(f32[3,3,128]{2,1,0:T(4,128)} %param.35) | copy-start | bytes 13828
  85.3 388.1 %copy-start.15 = (s32[3]{0:T(128)S(1)}, s32[3]{0:T(128)}, u32[]{:S(2)}) copy-start(s32[3]{0:T(128)} %param.37) | copy-start | bytes 40
  85.3 420.7 %copy-start.16 = (u32[32]{0:T(128)S(1)}, u32[32]{0:T(128)}, u32[]{:S(2)}) copy-start(u32[32]{0:T(128)} %constant.74) | copy-start | bytes 388
  85.3 421.3 %copy-start.1 = (f32[6,6,1024]{2,1,0:T(8,128)S(1)}, f32[6,6,1024]{2,1,0:T(8,128)}, u32[]{:S(2)}) copy-start(f32[6,6,1024]{2,1,0:T(8,128)} %param.32) | copy-start | bytes 442372
  85.3 421.3 %copy-start.10 = (f32[6]{0:T(128)S(1)}, f32[6]{0:T(128)}, u32[]{:S(2)}) copy-start(f32[6]{0:T(128)} %param.33) | copy-start | bytes 76
  472.5 35.3 %copy-start.7 = (f32[6,6]{1,0:T(8,128)S(1)}, f32[6,6]{1,0:T(8,128)}, u32[]{:S(2)}) copy-start(f32[6,6]{1,0:T(8,128)} %param.34) | copy-start | bytes 436
  472.5 36.0 %copy-start.5 = (f32[3,3,128]{2,1,0:T(4,128)S(1)}, f32[3,3,128]{2,1,0:T(4,128)}, u32[]{:S(2)}) copy-start(f32[3,3,128]{2,1,0:T(4,128)} %param.36) | copy-start | bytes 13828
  472.5 36.0 %copy-start.11 = (f32[3]{0:T(128)S(1)}, f32[3]{0:T(128)}, u32[]{:S(2)}) copy-start(f32[3]{0:T(128)} %constant.61.clone) | copy-start | bytes 40
where the time goes:
time: 510 us
  other arithmetic  386 us (76%)
  blocking collectives  111 us (22%)
  matrix products  6.47 us (1%)
    reduce_sum x16, other arithmetic, advance(): jnp.sum(kernel_value * (circulation[1][None, :] * sep_z - circulation[2][...  383 us
    unnamed x1, blocking collectives  31.7 us
    all_gather x1, blocking collectives, shards(): lax.all_gather(platform_vel, 'blk', axis=1, tiled=True)  23.2 us
    all_gather x1, blocking collectives, shards(): lax.all_gather(strengths, 'blk', axis=1, tiled=True)  18.8 us
    all_gather x1, blocking collectives, shards(): lax.all_gather(particle_pos, 'blk', axis=1, tiled=True)  18.8 us
    all_gather x1, blocking collectives, shards(): lax.all_gather(platform_pos, 'blk', axis=1, tiled=True)  18.7 us

commit v1 on v0

v1 whole, which is shorter than its diff:
```python
import functools
import math

import jax
import jax.numpy as jnp
import numpy as np
from jax import lax
from jax.experimental import pallas as pl
from jax.experimental.pallas import tpu as pltpu
from jax.sharding import PartitionSpec as P

core_square = 0.01
inverse_four_pi = 0.25 / math.pi
line_spacing = 1.0
rest_length = 0.95 * math.sqrt(1.36)
line_stiffness = 20.0
node_weight = 0.5
line_damping = 0.5
F32 = jnp.float32
BF16 = jnp.bfloat16
LANES = 128
TILE = 256
QUARTERS = 4
FEATURES = 32
third_turn = np.float32(2.0 * math.pi / 3.0)
cosines = [float(np.cos(third_turn * np.float32(k))) for k in range(3)]
sines = [float(np.sin(third_turn * np.float32(k))) for k in range(3)]


def piece(values):
    return values.astype(BF16).astype(F32)


def coordinate_pieces(pos, extra):
    first = jnp.round(pos * 64.0) * (1.0 / 64.0)
    rest = pos - first
    second = jnp.round(rest * 16384.0) * (1.0 / 16384.0)
    third = piece(rest - second)
    square = first * first
    norm = square[0:1] + square[1:2] + square[2:3]
    cross = rest * (pos + first)
    small = cross[0:1] + cross[1:2] + cross[2:3] + extra
    norm_a = piece(norm)
    norm_b = norm - norm_a
    small_a = piece(small)
    small_b = small - small_a
    return first, second, third, norm_a, norm_b, small_a, small_b


def source_rows(pos):
    first, second, third, norm_a, norm_b, small_a, small_b = coordinate_pieces(pos, 0.0)
    one = jnp.ones_like(norm_a)
    return jnp.concatenate(
        [first, norm_a, one, norm_b, one, small_a, one, first, second, small_b, one]
        + [second, first, third, second, third],
        axis=0,
    )


def target_rows(pos):
    first, second, third, norm_a, norm_b, small_a, small_b = coordinate_pieces(pos, core_square)
    one = jnp.ones_like(norm_a)
    first, second, third = -2.0 * first, -2.0 * second, -2.0 * third
    return jnp.concatenate(
        [first, one, norm_a, one, norm_b, one, small_a, second, first, one, small_b]
        + [second, third, first, third, second],
        axis=0,
    )


def strength_rows(block, scales):
    pos, vorticity, owner = block[0:3], block[3:6], block[6:7]
    scale = jnp.zeros_like(owner)
    for index, value in enumerate(scales):
        scale = jnp.where(owner == float(index), value, scale)
    strength = vorticity * scale
    s_hi = piece(strength)
    s_lo = piece(strength - s_hi)
    held = s_hi + s_lo
    moment = jnp.concatenate(
        [
            held[1:2] * pos[2:3] - held[2:3] * pos[1:2],
            held[2:3] * pos[0:1] - held[0:1] * pos[2:3],
            held[0:1] * pos[1:2] - held[1:2] * pos[0:1],
        ],
        axis=0,
    )
    m_hi = piece(moment)
    m_mid = piece(moment - m_hi)
    m_lo = moment - m_hi - m_mid
    return jnp.concatenate([s_hi, s_lo, m_hi, m_mid, m_lo, jnp.zeros_like(owner)], axis=0)


def step_kernel(
    chunk,
    me_ref,
    table_ref,
    thrust_ref,
    restoring_ref,
    mass_ref,
    line_platform_ref,
    misc_ref,
    pos_ref,
    blocks_ref,
    history_ref,
    memory_ref,
    offset_ref,
    line_velocity_ref,
    induced_ref,
    accel_ref,
    line_accel_ref,
    rows_ref,
    weights_ref,
    targets_ref,
    target_pos_ref,
    even_ref,
    odd_ref,
    sums_ref,
):
    devices = misc_ref.shape[0]
    platforms = thrust_ref.shape[0]
    blocks = blocks_ref.shape[0]
    own_count = pos_ref.shape[1]
    quarter = own_count // QUARTERS
    tiles = own_count // TILE + 1
    me = me_ref[0]

    on_platform = misc_ref[:, 7, :] == me.astype(F32)
    mark = on_platform.astype(F32)
    upper = lax.broadcasted_iota(jnp.int32, (LANES, LANES), 0) <= lax.broadcasted_iota(
        jnp.int32, (LANES, LANES), 1
    )
    counted = jnp.dot(mark.astype(BF16), upper.astype(F32).astype(BF16), preferred_element_type=F32)
    below = lax.broadcasted_iota(jnp.int32, (devices, devices), 0) > lax.broadcasted_iota(
        jnp.int32, (devices, devices), 1
    )
    totals = jnp.broadcast_to(counted[:, LANES - 1 :], counted.shape)
    before = jnp.dot(below.astype(F32).astype(BF16), totals.astype(BF16), preferred_element_type=F32)
    rank = jnp.where(on_platform, counted - 1.0 + before, -1.0)
    slots = lax.broadcasted_iota(jnp.int32, (LANES, LANES), 0).astype(F32)
    picked = jnp.zeros((24, LANES), F32)
    for device in range(devices):
        data = misc_ref[device, 0:8, :]
        hi = piece(data)
        mid = piece(data - hi)
        pieces = jnp.concatenate([hi, mid, data - hi - mid], axis=0).astype(BF16)
        pick = (slots == rank[device : device + 1]).astype(F32).astype(BF16)
        picked = picked + lax.dot_general(
            pieces, pick, (((1,), (1,)), ((), ())), preferred_element_type=F32
        )
    nodes = picked[0:8] + picked[8:16] + picked[16:24]
    current = jnp.concatenate([nodes[c : c + 1] + table_ref[0, c] for c in range(3)], axis=0)

    target_pos_ref[:, 0:own_count] = pos_ref[...]
    target_pos_ref[:, own_count : own_count + LANES] = current
    target_pos_ref[:, own_count + LANES :] = current
    for tile in range(tiles):
        features = target_rows(target_pos_ref[:, tile * TILE : (tile + 1) * TILE]).astype(BF16)
        for part in range(QUARTERS):
            slot = targets_ref.at[tile * QUARTERS + part]
            slot[...] = jnp.zeros((LANES, TILE), BF16)
            slot[part * FEATURES : (part + 1) * FEATURES, :] = features
        sums_ref[tile] = jnp.zeros((16, TILE), F32)

    scales = [
        thrust_ref[index] * (1.0 - table_ref[lax.bitwise_xor(me, index), 6])
        for index in range(platforms)
    ]

    def prepare(index, carry):
        block = blocks_ref[index]
        features = source_rows(block[0:3])
        stacked = jnp.concatenate(
            [features[:, part * quarter : (part + 1) * quarter] for part in range(QUARTERS)], axis=0
        )
        start = pl.multiple_of(index * quarter, quarter)
        rows_ref[pl.ds(start, quarter), :] = stacked.T.astype(BF16)
        strengths = strength_rows(block, scales).astype(BF16)
        for part in range(QUARTERS):
            weights_ref[part, :, pl.ds(start, quarter)] = strengths[
                :, part * quarter : (part + 1) * quarter
            ]
        return carry

    lax.fori_loop(0, blocks, prepare, 0)

    chunks = blocks * quarter // chunk
    steps = tiles * QUARTERS * chunks
    span = 256

    def distances(step, buffer):
        features = targets_ref[step // chunks]
        start = pl.multiple_of(step % chunks * chunk, chunk)
        for k in range(0, chunk, span):
            buffer[k : k + span, :] = jnp.dot(
                rows_ref[pl.ds(start + k, span), :], features, preferred_element_type=F32
            )

    def add_up(step, buffer):
        group = step // chunks
        start = pl.multiple_of(step % chunks * chunk, chunk)
        total = jnp.zeros((16, TILE), F32)
        for k in range(0, chunk, span):
            root = lax.rsqrt(buffer[k : k + span, :])
            pair = root * root * root
            high = pair.astype(BF16)
            low = (pair - high.astype(F32)).astype(BF16)
            weights = weights_ref[group % QUARTERS, :, pl.ds(start + k, span)]
            total = total + jnp.dot(weights, high, preferred_element_type=F32)
            total = total + jnp.dot(weights, low, preferred_element_type=F32)
        sums_ref[group // QUARTERS] += total

    distances(0, even_ref)

    def pairs(index, carry):
        step = 2 * index
        distances(step + 1, odd_ref)
        add_up(step, even_ref)
        distances(jnp.minimum(step + 2, steps - 1), even_ref)
        add_up(step + 1, odd_ref)
        return carry

    lax.fori_loop(0, steps // 2, pairs, 0)

    def velocity(tile):
        sums = sums_ref[tile]
        at = target_pos_ref[:, tile * TILE : (tile + 1) * TILE]
        a = [sums[c : c + 1] + sums[c + 3 : c + 4] for c in range(3)]
        b = [sums[c + 6 : c + 7] + sums[c + 9 : c + 10] + sums[c + 12 : c + 13] for c in range(3)]
        x = [at[c : c + 1] for c in range(3)]
        return [
            (a[1] * x[2] - a[2] * x[1] - b[0]) * inverse_four_pi,
            (a[2] * x[0] - a[0] * x[2] - b[1]) * inverse_four_pi,
            (a[0] * x[1] - a[1] * x[0] - b[2]) * inverse_four_pi,
        ]

    for tile in range(tiles - 1):
        induced_ref[:, tile * TILE : (tile + 1) * TILE] = jnp.concatenate(velocity(tile), axis=0)

    wind = [row[:, 0:LANES] for row in velocity(tiles - 1)]
    arm = [nodes[3 + c : 4 + c] for c in range(3)]
    turn = [table_ref[0, 9 + c] for c in range(3)]
    rigid = [
        table_ref[0, 6] + (turn[1] * arm[2] - turn[2] * arm[1]),
        table_ref[0, 7] + (turn[2] * arm[0] - turn[0] * arm[2]),
        table_ref[0, 8] + (turn[0] * arm[1] - turn[1] * arm[0]),
    ]
    relative = [1.0 + wind[0] - rigid[0], wind[1] - rigid[1], wind[2] - rigid[2]]
    magnitude = jnp.sqrt(
        relative[0] * relative[0] + relative[1] * relative[1] + relative[2] * relative[2]
    )
    force = [nodes[6:7] * magnitude * row for row in relative]
    moment = [
        arm[1] * force[2] - arm[2] * force[1],
        arm[2] * force[0] - arm[0] * force[2],
        arm[0] * force[1] - arm[1] * force[0],
    ]
    loads = [jnp.sum(row, axis=1, keepdims=True) for row in force + moment]

    lines = offset_ref.shape[1]
    segments = offset_ref.shape[2]

    def headings(number):
        which = lax.rem(number, 3)
        pick = lambda values: jnp.where(
            which == 0, values[0], jnp.where(which == 1, values[1], values[2])
        )
        return [pick(cosines), pick(sines), jnp.full(number.shape, 0.6, F32)]

    shape = (lines, segments)
    row_index = lax.broadcasted_iota(jnp.int32, shape, 0)
    node_index = lax.broadcasted_iota(jnp.int32, shape, 1)
    heading = headings(me * lines + row_index)
    depth = (segments - node_index).astype(F32)
    points = [-line_spacing * heading[c] * depth + offset_ref[c] for c in range(3)]
    fair = [jnp.zeros(shape, F32)] * 3
    for line in range(lines):
        owner = lax.bitwise_xor(me, line_platform_ref[line])
        fair = [jnp.where(row_index == line, table_ref[owner, c], fair[c]) for c in range(3)]
    last = node_index == segments - 1
    following = [
        jnp.where(last, fair[c], pltpu.roll(points[c], segments - 1, 1)) for c in range(3)
    ]

    def pulls(segment):
        length = jnp.sqrt(
            segment[0] * segment[0] + segment[1] * segment[1] + segment[2] * segment[2]
        )
        tension = line_stiffness * (length - rest_length) / rest_length
        return [tension / length * part for part in segment]

    pull = pulls([following[c] - points[c] for c in range(3)])
    for c in range(3):
        previous = jnp.where(node_index == 0, 0.0, pltpu.roll(pull[c], 1, 1))
        gravity = -node_weight if c == 2 else 0.0
        acceleration = pull[c] - previous + gravity - line_damping * line_velocity_ref[c]
        line_accel_ref[c] = jnp.where(node_index == 0, 0.0, acceleration)

    shape = (devices, LANES)
    sender = lax.bitwise_xor(lax.broadcasted_iota(jnp.int32, shape, 0), jnp.full(shape, me))
    number = lax.broadcasted_iota(jnp.int32, shape, 1)
    heading = headings(sender * lines + number)
    ends = [
        table_ref[0, c] - (-line_spacing * heading[c] + misc_ref[:, 9 + c, :]) for c in range(3)
    ]
    ours = jnp.logical_and(number < lines, misc_ref[:, 12, :] == me.astype(F32))
    pull = pulls(ends)
    for c in range(3):
        taken = jnp.where(ours, pull[c], 0.0)
        loads[c] = loads[c] - jnp.sum(jnp.sum(taken, axis=0, keepdims=True), axis=1, keepdims=True)

    history = history_ref[0]
    total = []
    for i in range(6):
        product = jnp.sum(memory_ref[i] * history, axis=0, keepdims=True)
        radiation = -jnp.sum(product, axis=1, keepdims=True)
        total.append(loads[i] + radiation - restoring_ref[i] * table_ref[0, i])
    for i in range(6):
        value = mass_ref[i, 0] * total[0]
        for j in range(1, 6):
            value = value + mass_ref[i, j] * total[j]
        accel_ref[i : i + 1, :] = value


def shards(
    particle_pos,
    vorticity,
    particle_owner,
    thrust_coef,
    node_pos,
    lever_arm,
    chord_coef,
    node_platform,
    platform_pos,
    platform_vel,
    velocity_history,
    memory_kernel,
    restoring,
    inverse_mass,
    line_offset,
    line_velocity,
    line_platform,
):
    devices = lax.axis_size("blk")
    me = lax.axis_index("blk")
    own_count = particle_pos.shape[1]
    lines, segments = line_offset.shape[1:]

    def wide(rows):
        return jnp.pad(rows, ((0, 0), (0, LANES - rows.shape[1])))

    motion = jnp.concatenate([platform_pos, platform_vel], axis=0).reshape(1, 12)
    misc = jnp.concatenate(
        [
            node_pos,
            lever_arm,
            chord_coef[None],
            node_platform.astype(F32)[None],
            wide(motion),
            wide(line_offset[:, :, segments - 1]),
            wide(line_platform.astype(F32)[None]),
            jnp.zeros((3, LANES), F32),
        ],
        axis=0,
    )[None]
    own = jnp.concatenate(
        [
            particle_pos,
            vorticity,
            particle_owner.astype(F32)[None],
            jnp.zeros((1, own_count), F32),
        ],
        axis=0,
    )[None]

    def swap(values, distance):
        return lax.ppermute(values, "blk", [(i, i ^ distance) for i in range(devices)])

    distance = 1
    while distance < devices:
        misc = jnp.concatenate([misc, swap(misc, distance)], axis=0)
        distance *= 2
    received = [own] + [swap(own, distance) for distance in range(2, devices, 2)]
    half = jnp.concatenate(received, axis=0)
    blocks = jnp.concatenate([half, swap(half, 1)], axis=0)

    table = misc[:, 8, 0:16]
    tiles = own_count // TILE + 1
    rows = devices * own_count // QUARTERS
    chunk = min(rows, 4096)
    smem = pl.BlockSpec(memory_space=pltpu.SMEM)
    vmem = pl.BlockSpec(memory_space=pltpu.VMEM)
    return pl.pallas_call(
        functools.partial(step_kernel, chunk),
        in_specs=[smem] * 6 + [vmem] * 7,
        out_specs=(vmem,) * 3,
        out_shape=(
            jax.ShapeDtypeStruct(particle_pos.shape, F32),
            jax.ShapeDtypeStruct(platform_pos.shape, F32),
            jax.ShapeDtypeStruct(line_offset.shape, F32),
        ),
        scratch_shapes=[
            pltpu.VMEM((rows, LANES), BF16),
            pltpu.VMEM((QUARTERS, 16, rows), BF16),
            pltpu.VMEM((tiles * QUARTERS, LANES, TILE), BF16),
            pltpu.VMEM((3, tiles * TILE), F32),
            pltpu.VMEM((chunk, TILE), F32),
            pltpu.VMEM((chunk, TILE), F32),
            pltpu.VMEM((tiles, 16, TILE), F32),
        ],
        compiler_params=pltpu.CompilerParams(vmem_limit_bytes=56 * 2**20),
        name="coupled_step",
    )(
        me.astype(jnp.int32)[None],
        table,
        thrust_coef,
        restoring,
        inverse_mass,
        line_platform,
        misc,
        particle_pos,
        blocks,
        velocity_history,
        memory_kernel,
        line_offset,
        line_velocity,
    )


def solution(mesh):
    return jax.shard_map(
        shards,
        mesh=mesh,
        in_specs=(
            P(None, ("farm", "blk")),
            P(None, ("farm", "blk")),
            P(("farm", "blk")),
            P("farm"),
            P(None, ("farm", "blk")),
            P(None, ("farm", "blk")),
            P(("farm", "blk")),
            P(("farm", "blk")),
            P(None, ("farm", "blk")),
            P(None, ("farm", "blk")),
            P(("farm", "blk"), None, None),
            P(),
            P(),
            P(),
            P(None, ("farm", "blk"), None),
            P(None, ("farm", "blk"), None),
            P(("farm", "blk")),
        ),
        out_specs=(
            P(None, ("farm", "blk")),
            P(None, ("farm", "blk")),
            P(None, ("farm", "blk"), None),
        ),
        check_vma=False,
    )
```

time: 510 us -> 134 us (0.26)
  other arithmetic: 386 us -> 1.66 us
  blocking collectives: 111 us -> 0 us
  Pallas kernels: 0 us -> 95.3 us
  starting transfers between devices: 0 us -> 18.1 us
  waiting for transfers between devices: 0 us -> 11 us
  matrix products: 6.47 us -> 0 us
    reduce_sum x18 -> x0, other arithmetic: 383 us -> none  [the longest x16 383 us: advance(): jnp.sum(kernel_value * (circulation[1][None, :] * sep_z - circulation[2][...]
    pallas_call x0 -> x1, Pallas kernels: none -> 95.3 us  [shards(): pl.pallas_call(functools.partial(step_kernel, chunk), in_specs=[smem] * 6...]
    all_gather x4 -> x0, blocking collectives: 79.6 us -> none  [the longest x1 23.2 us: shards(): lax.all_gather(platform_vel, 'blk', axis=1, tiled=True)]
    unnamed x1 -> x0, blocking collectives: 31.7 us -> none
    ppermute x0 -> x12, starting transfers between devices: none -> 18.1 us  [swap(): lax.ppermute(values, 'blk', [(i, i ^ distance) for i in range(devices)])]
    ppermute x0 -> x12, waiting for transfers between devices: none -> 11 us  [swap(): lax.ppermute(values, 'blk', [(i, i ^ distance) for i in range(devices)])]
    dot_general x9 -> x0, matrix products: 6.47 us -> none  [the longest x1 1.45 us: shards(): owner_thrust = jnp.dot(owner_hot, thrust_coef, precision=high_precision)]
  transfers between devices with their start and end apart: 0 -> 12, of which waited for: 0 -> 4; matrix products, arithmetic and copies ran while one was open for 0% -> 1% of each run, Pallas kernels for 0% -> 0%
where the time goes in v1:
time: 134 us
  Pallas kernels  95.3 us (71%)
  starting transfers between devices  18.1 us (14%)
  waiting for transfers between devices  11 us (8%)
  local copies, waits for them, and re-layouts  7.28 us (5%)
  other arithmetic  1.66 us (1%)
    pallas_call x1, Pallas kernels, shards(): pl.pallas_call(functools.partial(step_kernel, chunk), in_specs=[smem] * 6...  95.3 us
    ppermute x12, starting transfers between devices, swap(): lax.ppermute(values, 'blk', [(i, i ^ distance) for i in range(devices)])  18.1 us
    ppermute x12, waiting for transfers between devices, swap(): lax.ppermute(values, 'blk', [(i, i ^ distance) for i in range(devices)])  11 us
    unnamed x34, local copies, waits for them, and re-layouts  5.04 us
  transfers between devices with their start and end apart: 12, of which 4 were waited for; matrix products, arithmetic and copies ran while one was open for 1% of the time, Pallas kernels for 0%

profile of v1, /device:TPU:0, one launch (start us, length us, event | category | flops | bytes accessed | tf_op | source)
XLA Modules:
  0.0 134.1 jit_solution(16792836993704568996)
XLA Ops:
  0.6 0.7 convert_element_type.17
  1.3 0.1 pad.18.clone
  1.4 0.0 copy-start.2
  1.4 0.9 constant_dynamic-update-slice_fusion.12
  2.3 3.0 %collective-permute-start.4 = (f32[1,8,2048]{2,1,0:T(8,128)S(1)}, f32[1,8,2048]{2,1,0:T(8,128)S(1)}, u32[]{:S(2)}, u32[]{:S(2)}) collective-permute-start(f32[1,8,2048]{2,1,0:T(8,128)S(1)} %get-tuple-element.10), channel_id=1, source_target_pairs={{0,2},{1,3},{2,0},{3,1},{4,6},{5,7},{6,4},{7,5},{8,10},{9,11},{10,... | collective-permute-start | bytes 196616 | tf_op jit(solution)/shard_map/ppermute | solution.py:377
  5.3 1.6 %collective-permute-start.5 = (f32[1,8,2048]{2,1,0:T(8,128)S(1)}, f32[1,8,2048]{2,1,0:T(8,128)S(1)}, u32[]{:S(2)}, u32[]{:S(2)}) collective-permute-start(f32[1,8,2048]{2,1,0:T(8,128)S(1)} %get-tuple-element.10), channel_id=1, source_target_pairs={{0,4},{1,5},{2,6},{3,7},{4,0},{5,1},{6,2},{7,3},{8,12},{9,13},{10,... | collective-permute-start | bytes 196616 | tf_op jit(solution)/shard_map/ppermute | solution.py:377
  6.9 0.0 collective-permute-start.6
  6.9 3.0 %collective-permute-start.7 = (f32[1,8,2048]{2,1,0:T(8,128)S(1)}, f32[1,8,2048]{2,1,0:T(8,128)S(1)}, u32[]{:S(2)}, u32[]{:S(2)}) collective-permute-start(f32[1,8,2048]{2,1,0:T(8,128)S(1)} %get-tuple-element.10), channel_id=1, source_target_pairs={{0,8},{1,9},{2,10},{3,11},{4,12},{5,13},{6,14},{7,15},{8,0},{9,1},... | collective-permute-start | bytes 196616 | tf_op jit(solution)/shard_map/ppermute | solution.py:377
  9.9 0.0 copy-done.2
  9.9 0.2 slice_reduce_fusion
  10.0 0.0 copy-start.8
  10.0 0.0 copy-start.9
  10.0 0.6 copy-done.8
  10.7 0.0 copy-done.9
  10.7 0.1 maximum_bitcast_fusion.1
  10.8 0.0 copy-start.6
  10.8 0.6 copy-done.6
  11.4 0.0 copy-start.10
  11.4 0.6 copy-done.10
  12.1 0.0 copy-start.7
  12.1 0.0 copy-start.4
  12.1 0.0 copy-start.5
  12.1 0.6 copy-done.7
  12.7 0.0 copy-done.4
  12.8 0.0 copy-done.5
  12.8 0.1 collective-permute-start
  12.9 0.0 copy-start.3
  13.0 0.7 copy-done.3
  13.7 0.6 copy.22.history_ref
  14.3 0.0 collective-permute-done
  14.3 1.3 collective-permute-start.8
  15.6 0.0 collective-permute-done.4
  15.6 3.7 %collective-permute-start.9 = (f32[1,8,2048]{2,1,0:T(8,128)S(1)}, f32[1,8,2048]{2,1,0:T(8,128)S(1)}, u32[]{:S(2)}, u32[]{:S(2)}) collective-permute-start(f32[1,8,2048]{2,1,0:T(8,128)S(1)} %get-tuple-element.10), channel_id=1, source_target_pairs={{0,12},{1,13},{2,14},{3,15},{4,8},{5,9},{6,10},{7,11},{8,4},{9,5},... | collective-permute-start | bytes 196616 | tf_op jit(solution)/shard_map/ppermute | solution.py:377
  19.2 0.0 collective-permute-done.5
  19.3 0.1 collective-permute-start.10
  19.4 0.0 collective-permute-done.6
  19.4 1.7 %collective-permute-start.1 = (f32[2,16,128]{2,1,0:T(8,128)S(1)}, f32[2,16,128]{2,1,0:T(8,128)S(1)}, u32[]{:S(2)}, u32[]{:S(2)}) collective-permute-start(f32[2,16,128]{2,1,0:T(8,128)S(1)} %pad_maximum_fusion.2), channel_id=1, source_target_pairs={{0,2},{1,3},{2,0},{3,1},{4,6},{5,7},{6,4},{7,5},{8,10},{9,11},{10,... | collective-permute-start | bytes 49160 | tf_op jit(solution)/shard_map/ppermute | solution.py:377
  21.1 0.0 collective-permute-done.7
  21.1 2.6 %collective-permute-done.8 = f32[1,8,2048]{2,1,0:T(8,128)S(1)} collective-permute-done((f32[1,8,2048]{2,1,0:T(8,128)S(1)}, f32[1,8,2048]{2,1,0:T(8,128)S(1)}, u32[]{:S(2)}, u32[]{:S(2)}) %collective-permute-start.8) | collective-permute-done | bytes 65568 | tf_op jit(solution)/shard_map/ppermute | solution.py:377
  23.8 0.0 collective-permute-done.9
  23.8 2.5 %collective-permute-done.10 = f32[1,8,2048]{2,1,0:T(8,128)S(1)} collective-permute-done((f32[1,8,2048]{2,1,0:T(8,128)S(1)}, f32[1,8,2048]{2,1,0:T(8,128)S(1)}, u32[]{:S(2)}, u32[]{:S(2)}) %collective-permute-start.10) | collective-permute-done | bytes 65568 | tf_op jit(solution)/shard_map/ppermute | solution.py:377
  26.3 0.1 collective-permute-start.11
  26.4 0.0 collective-permute-done.1
  26.4 1.9 %collective-permute-start.2 = (f32[4,16,128]{2,1,0:T(8,128)S(1)}, f32[4,16,128]{2,1,0:T(8,128)S(1)}, u32[]{:S(2)}, u32[]{:S(2)}) collective-permute-start(f32[4,16,128]{2,1,0:T(8,128)S(1)} %pad_maximum_fusion.1), channel_id=1, source_target_pairs={{0,4},{1,5},{2,6},{3,7},{4,0},{5,1},{6,2},{7,3},{8,12},{9,13},{10,... | collective-permute-start | bytes 98312 | tf_op jit(solution)/shard_map/ppermute | solution.py:377
  28.3 2.1 %collective-permute-done.2 = f32[4,16,128]{2,1,0:T(8,128)S(1)} collective-permute-done((f32[4,16,128]{2,1,0:T(8,128)S(1)}, f32[4,16,128]{2,1,0:T(8,128)S(1)}, u32[]{:S(2)}, u32[]{:S(2)}) %collective-permute-start.2) | collective-permute-done | bytes 32800 | tf_op jit(solution)/shard_map/ppermute | solution.py:377
  30.4 1.7 %collective-permute-start.3 = (f32[8,16,128]{2,1,0:T(8,128)S(1)}, f32[8,16,128]{2,1,0:T(8,128)S(1)}, u32[]{:S(2)}, u32[]{:S(2)}) collective-permute-start(f32[8,16,128]{2,1,0:T(8,128)S(1)} %pad_maximum_fusion), channel_id=1, source_target_pairs={{0,8},{1,9},{2,10},{3,11},{4,12},{5,13},{6,14},{7,15},{8,0},{9,1},... | collective-permute-start | bytes 196616 | tf_op jit(solution)/shard_map/ppermute | solution.py:377
  32.0 3.8 %collective-permute-done.3 = f32[8,16,128]{2,1,0:T(8,128)S(1)} collective-permute-done((f32[8,16,128]{2,1,0:T(8,128)S(1)}, f32[8,16,128]{2,1,0:T(8,128)S(1)}, u32[]{:S(2)}, u32[]{:S(2)}) %collective-permute-start.3) | collective-permute-done | bytes 65568 | tf_op jit(solution)/shard_map/ppermute | solution.py:377
  35.9 0.0 copy-start.1
  35.9 0.6 slice.8
  36.5 0.0 collective-permute-done.11
  36.6 0.0 copy-done.1
  36.6 0.0 copy-start
  36.6 1.0 copy-done
  37.6 95.3 %coupled_step.1 = (f32[3,2048]{1,0:T(4,128)}, f32[6,1]{1,0:T(8,128)}, f32[3,3,128]{2,1,0:T(4,128)}) custom-call(s32[1]{0:T(128)} %bitcast.me_ref, f32[16,16]{1,0:T(8,128)} %bitcast.20, f32[16]{0:T(128)} %thrust_ref.1, f32[6]{0:T(128)} %restoring_ref.1, f32[6,6]{1,0:T(8,128)} %mass_ref.1, s32[3]{0:T(128)} %line_platform_ref.1, f32[16,16,128]{2,1,0:T(8,128)} %copy-done.1, ...), custom_call_target="tpu_custom_call" | custom-call | tf_op jit(solution)/shard_map/coupled_step/pallas_call | solution.py:393
  132.8 1.3 copy.23
  (24 shorter events, 0.2 us)
Async XLA Ops:
  1.4 8.5 %copy-start.2 = (f32[3,3,128]{2,1,0:T(4,128)S(1)}, f32[3,3,128]{2,1,0:T(4,128)}, u32[]{:S(2)}) copy-start(f32[3,3,128]{2,1,0:T(4,128)} %offset_ref.1) | copy-start | bytes 13828
  2.3 13.3 %collective-permute-start.4 = (f32[1,8,2048]{2,1,0:T(8,128)S(1)}, f32[1,8,2048]{2,1,0:T(8,128)S(1)}, u32[]{:S(2)}, u32[]{:S(2)}) collective-permute-start(f32[1,8,2048]{2,1,0:T(8,128)S(1)} %get-tuple-element.10), channel_id=1, source_target_pairs={{0,2},{1,3},{2,0},{3,1},{4,6},{5,7},{6,4},{7,5},{8,10},{9,11},{10,... | collective-permute-start | bytes 196616 | tf_op jit(solution)/shard_map/ppermute | solution.py:377
  5.3 13.9 %collective-permute-start.5 = (f32[1,8,2048]{2,1,0:T(8,128)S(1)}, f32[1,8,2048]{2,1,0:T(8,128)S(1)}, u32[]{:S(2)}, u32[]{:S(2)}) collective-permute-start(f32[1,8,2048]{2,1,0:T(8,128)S(1)} %get-tuple-element.10), channel_id=1, source_target_pairs={{0,4},{1,5},{2,6},{3,7},{4,0},{5,1},{6,2},{7,3},{8,12},{9,13},{10,... | collective-permute-start | bytes 196616 | tf_op jit(solution)/shard_map/ppermute | solution.py:377
  6.9 12.5 %collective-permute-start.6 = (f32[1,8,2048]{2,1,0:T(8,128)S(1)}, f32[1,8,2048]{2,1,0:T(8,128)S(1)}, u32[]{:S(2)}, u32[]{:S(2)}) collective-permute-start(f32[1,8,2048]{2,1,0:T(8,128)S(1)} %get-tuple-element.10), channel_id=1, source_target_pairs={{0,6},{1,7},{2,4},{3,5},{4,2},{5,3},{6,0},{7,1},{8,14},{9,15},{10,... | collective-permute-start | bytes 196616 | tf_op jit(solution)/shard_map/ppermute | solution.py:377
  6.9 14.2 %collective-permute-start.7 = (f32[1,8,2048]{2,1,0:T(8,128)S(1)}, f32[1,8,2048]{2,1,0:T(8,128)S(1)}, u32[]{:S(2)}, u32[]{:S(2)}) collective-permute-start(f32[1,8,2048]{2,1,0:T(8,128)S(1)} %get-tuple-element.10), channel_id=1, source_target_pairs={{0,8},{1,9},{2,10},{3,11},{4,12},{5,13},{6,14},{7,15},{8,0},{9,1},... | collective-permute-start | bytes 196616 | tf_op jit(solution)/shard_map/ppermute | solution.py:377
  10.0 0.7 copy-start.8
  10.0 0.7 copy-start.9
  10.8 0.7 copy-start.6
  11.4 0.7 copy-start.10
  12.1 0.7 copy-start.7
  12.1 0.7 copy-start.4
  12.1 0.7 copy-start.5
  12.8 1.4 %collective-permute-start = (f32[1,16,128]{2,1,0:T(8,128)S(1)}, f32[1,16,128]{2,1,0:T(8,128)S(1)}, u32[]{:S(2)}, u32[]{:S(2)}) collective-permute-start(f32[1,16,128]{2,1,0:T(8,128)S(1)} %bitcast.16), channel_id=1, source_target_pairs={{0,1},{1,0},{2,3},{3,2},{4,5},{5,4},{6,7},{7,6},{8,9},{9,8},{10,11... | collective-permute-start | bytes 24584 | tf_op jit(solution)/shard_map/ppermute | solution.py:377
  12.9 0.7 copy-start.3
  14.3 9.5 %collective-permute-start.8 = (f32[1,8,2048]{2,1,0:T(8,128)S(1)}, f32[1,8,2048]{2,1,0:T(8,128)S(1)}, u32[]{:S(2)}, u32[]{:S(2)}) collective-permute-start(f32[1,8,2048]{2,1,0:T(8,128)S(1)} %get-tuple-element.10), channel_id=1, source_target_pairs={{0,10},{1,11},{2,8},{3,9},{4,14},{5,15},{6,12},{7,13},{8,2},{9,3},... | collective-permute-start | bytes 196616 | tf_op jit(solution)/shard_map/ppermute | solution.py:377
  15.6 8.2 %collective-permute-start.9 = (f32[1,8,2048]{2,1,0:T(8,128)S(1)}, f32[1,8,2048]{2,1,0:T(8,128)S(1)}, u32[]{:S(2)}, u32[]{:S(2)}) collective-permute-start(f32[1,8,2048]{2,1,0:T(8,128)S(1)} %get-tuple-element.10), channel_id=1, source_target_pairs={{0,12},{1,13},{2,14},{3,15},{4,8},{5,9},{6,10},{7,11},{8,4},{9,5},... | collective-permute-start | bytes 196616 | tf_op jit(solution)/shard_map/ppermute | solution.py:377
  19.3 7.0 %collective-permute-start.10 = (f32[1,8,2048]{2,1,0:T(8,128)S(1)}, f32[1,8,2048]{2,1,0:T(8,128)S(1)}, u32[]{:S(2)}, u32[]{:S(2)}) collective-permute-start(f32[1,8,2048]{2,1,0:T(8,128)S(1)} %get-tuple-element.10), channel_id=1, source_target_pairs={{0,14},{1,15},{2,12},{3,13},{4,10},{5,11},{6,8},{7,9},{8,6},{9,7},... | collective-permute-start | bytes 196616 | tf_op jit(solution)/shard_map/ppermute | solution.py:377
  19.4 7.0 %collective-permute-start.1 = (f32[2,16,128]{2,1,0:T(8,128)S(1)}, f32[2,16,128]{2,1,0:T(8,128)S(1)}, u32[]{:S(2)}, u32[]{:S(2)}) collective-permute-start(f32[2,16,128]{2,1,0:T(8,128)S(1)} %pad_maximum_fusion.2), channel_id=1, source_target_pairs={{0,2},{1,3},{2,0},{3,1},{4,6},{5,7},{6,4},{7,5},{8,10},{9,11},{10,... | collective-permute-start | bytes 49160 | tf_op jit(solution)/shard_map/ppermute | solution.py:377
  26.3 10.2 %collective-permute-start.11 = (f32[8,8,2048]{2,1,0:T(8,128)S(1)}, f32[8,8,2048]{2,1,0:T(8,128)S(1)}, u32[]{:S(2)}, u32[]{:S(2)}) collective-permute-start(f32[8,8,2048]{2,1,0:T(8,128)S(1)} %get-tuple-element.11), channel_id=1, source_target_pairs={{0,1},{1,0},{2,3},{3,2},{4,5},{5,4},{6,7},{7,6},{8,9},{9,8},{10,11... | collective-permute-start | bytes 1572872 | tf_op jit(solution)/shard_map/ppermute | solution.py:377
  26.4 4.0 %collective-permute-start.2 = (f32[4,16,128]{2,1,0:T(8,128)S(1)}, f32[4,16,128]{2,1,0:T(8,128)S(1)}, u32[]{:S(2)}, u32[]{:S(2)}) collective-permute-start(f32[4,16,128]{2,1,0:T(8,128)S(1)} %pad_maximum_fusion.1), channel_id=1, source_target_pairs={{0,4},{1,5},{2,6},{3,7},{4,0},{5,1},{6,2},{7,3},{8,12},{9,13},{10,... | collective-permute-start | bytes 98312 | tf_op jit(solution)/shard_map/ppermute | solution.py:377
  30.4 5.5 %collective-permute-start.3 = (f32[8,16,128]{2,1,0:T(8,128)S(1)}, f32[8,16,128]{2,1,0:T(8,128)S(1)}, u32[]{:S(2)}, u32[]{:S(2)}) collective-permute-start(f32[8,16,128]{2,1,0:T(8,128)S(1)} %pad_maximum_fusion), channel_id=1, source_target_pairs={{0,8},{1,9},{2,10},{3,11},{4,12},{5,13},{6,14},{7,15},{8,0},{9,1},... | collective-permute-start | bytes 196616 | tf_op jit(solution)/shard_map/ppermute | solution.py:377
  35.9 0.7 copy-start.1
  36.6 1.0 copy-start

commit v2 on v1

v2 whole, which is shorter than its diff:
```python
import functools
import math

import jax
import jax.numpy as jnp
import numpy as np
from jax import lax
from jax.experimental import pallas as pl
from jax.experimental.pallas import tpu as pltpu
from jax.sharding import PartitionSpec as P

core_square = 0.01
inverse_four_pi = 0.25 / math.pi
line_spacing = 1.0
rest_length = 0.95 * math.sqrt(1.36)
line_stiffness = 20.0
node_weight = 0.5
line_damping = 0.5
F32 = jnp.float32
BF16 = jnp.bfloat16
LANES = 128
TILE = 256
QUARTERS = 4
FEATURES = 32
SPAN = 256
third_turn = np.float32(2.0 * math.pi / 3.0)
cosines = [float(np.cos(third_turn * np.float32(k))) for k in range(3)]
sines = [float(np.sin(third_turn * np.float32(k))) for k in range(3)]


def piece(values):
    return values.astype(BF16).astype(F32)


def coordinate_pieces(pos, extra):
    first = jnp.round(pos * 64.0) * (1.0 / 64.0)
    rest = pos - first
    second = jnp.round(rest * 16384.0) * (1.0 / 16384.0)
    third = piece(rest - second)
    square = first * first
    norm = square[0:1] + square[1:2] + square[2:3]
    cross = rest * (pos + first)
    small = cross[0:1] + cross[1:2] + cross[2:3] + extra
    norm_a = piece(norm)
    norm_b = norm - norm_a
    small_a = piece(small)
    small_b = small - small_a
    return first, second, third, norm_a, norm_b, small_a, small_b


def source_rows(pos):
    first, second, third, norm_a, norm_b, small_a, small_b = coordinate_pieces(pos, 0.0)
    one = jnp.ones_like(norm_a)
    return jnp.concatenate(
        [first, norm_a, one, norm_b, one, small_a, one, first, second, small_b, one]
        + [second, first, third, second, third],
        axis=0,
    )


def target_rows(pos):
    first, second, third, norm_a, norm_b, small_a, small_b = coordinate_pieces(pos, core_square)
    one = jnp.ones_like(norm_a)
    first, second, third = -2.0 * first, -2.0 * second, -2.0 * third
    return jnp.concatenate(
        [first, one, norm_a, one, norm_b, one, small_a, second, first, one, small_b]
        + [second, third, first, third, second],
        axis=0,
    )


def strength_rows(block, scales):
    pos, vorticity, owner = block[0:3], block[3:6], block[6:7]
    scale = jnp.zeros_like(owner)
    for index, value in enumerate(scales):
        scale = jnp.where(owner == float(index), value, scale)
    strength = vorticity * scale
    s_hi = piece(strength)
    s_lo = piece(strength - s_hi)
    held = s_hi + s_lo
    moment = jnp.concatenate(
        [
            held[1:2] * pos[2:3] - held[2:3] * pos[1:2],
            held[2:3] * pos[0:1] - held[0:1] * pos[2:3],
            held[0:1] * pos[1:2] - held[1:2] * pos[0:1],
        ],
        axis=0,
    )
    m_hi = piece(moment)
    m_mid = piece(moment - m_hi)
    m_lo = moment - m_hi - m_mid
    return jnp.concatenate([s_hi, s_lo, m_hi, m_mid, m_lo, jnp.zeros_like(owner)], axis=0)


def strength_scales(me, table_ref, thrust_ref):
    return [
        thrust_ref[index] * (1.0 - table_ref[lax.bitwise_xor(me, index), 6])
        for index in range(thrust_ref.shape[0])
    ]


def pair_sums(block_refs, scales, target_pos_ref, sums_ref, scratch):
    rows_ref, weights_ref, targets_ref, even_ref, odd_ref = scratch
    quarter = block_refs[0].shape[2] // QUARTERS
    tiles = sums_ref.shape[0]
    for tile in range(tiles):
        features = target_rows(target_pos_ref[:, tile * TILE : (tile + 1) * TILE]).astype(BF16)
        for part in range(QUARTERS):
            slot = targets_ref.at[tile * QUARTERS + part]
            slot[...] = jnp.zeros((LANES, TILE), BF16)
            slot[part * FEATURES : (part + 1) * FEATURES, :] = features

    first = 0
    for block_ref in block_refs:

        def prepare(index, carry, block_ref=block_ref, first=first):
            block = block_ref[index]
            features = source_rows(block[0:3])
            stacked = jnp.concatenate(
                [features[:, part * quarter : (part + 1) * quarter] for part in range(QUARTERS)],
                axis=0,
            )
            start = pl.multiple_of((first + index) * quarter, quarter)
            rows_ref[pl.ds(start, quarter), :] = stacked.T.astype(BF16)
            strengths = strength_rows(block, scales).astype(BF16)
            for part in range(QUARTERS):
                weights_ref[part, :, pl.ds(start, quarter)] = strengths[
                    :, part * quarter : (part + 1) * quarter
                ]
            return carry

        lax.fori_loop(0, block_ref.shape[0], prepare, 0)
        first += block_ref.shape[0]

    reach = even_ref.shape[0] // QUARTERS
    chunks = rows_ref.shape[0] // reach
    steps = tiles * chunks
    span = min(SPAN, reach)

    def distances(step, buffer):
        tile = step // chunks
        start = pl.multiple_of(step % chunks * reach, reach)
        for part in range(QUARTERS):
            features = targets_ref[tile * QUARTERS + part]
            for k in range(0, reach, span):
                at = part * reach + k
                buffer[at : at + span, :] = jnp.dot(
                    rows_ref[pl.ds(start + k, span), :], features, preferred_element_type=F32
                )

    def add_up(step, buffer):
        tile = step // chunks
        start = pl.multiple_of(step % chunks * reach, reach)
        total = jnp.zeros((16, TILE), F32)
        for part in range(QUARTERS):
            for k in range(0, reach, span):
                at = part * reach + k
                root = lax.rsqrt(buffer[at : at + span, :])
                pair = root * root * root
                high = pair.astype(BF16)
                low = (pair - high.astype(F32)).astype(BF16)
                weights = weights_ref[part, :, pl.ds(start + k, span)]
                total = total + jnp.dot(weights, high, preferred_element_type=F32)
                total = total + jnp.dot(weights, low, preferred_element_type=F32)
        sums_ref[tile] += total

    def two_steps(index, carry):
        step = 2 * index
        distances(step + 1, odd_ref)
        add_up(step, even_ref)
        distances(step + 2, even_ref)
        add_up(step + 1, odd_ref)
        return carry

    distances(0, even_ref)
    doubles = (steps - 1) // 2
    lax.fori_loop(0, doubles, two_steps, 0)
    if steps % 2 == 0:
        distances(steps - 1, odd_ref)
        add_up(steps - 2, even_ref)
        add_up(steps - 1, odd_ref)
    else:
        add_up(steps - 1, even_ref)


def platform_nodes(me, misc_ref):
    devices = misc_ref.shape[0]
    on_platform = misc_ref[:, 7, :] == me.astype(F32)
    mark = on_platform.astype(F32)
    upper = lax.broadcasted_iota(jnp.int32, (LANES, LANES), 0) <= lax.broadcasted_iota(
        jnp.int32, (LANES, LANES), 1
    )
    counted = jnp.dot(mark.astype(BF16), upper.astype(F32).astype(BF16), preferred_element_type=F32)
    below = lax.broadcasted_iota(jnp.int32, (devices, devices), 0) > lax.broadcasted_iota(
        jnp.int32, (devices, devices), 1
    )
    totals = jnp.broadcast_to(counted[:, LANES - 1 :], counted.shape)
    before = jnp.dot(below.astype(F32).astype(BF16), totals.astype(BF16), preferred_element_type=F32)
    rank = jnp.where(on_platform, counted - 1.0 + before, -1.0)
    slots = lax.broadcasted_iota(jnp.int32, (LANES, LANES), 0).astype(F32)
    picked = jnp.zeros((24, LANES), F32)
    for device in range(devices):
        data = misc_ref[device, 0:8, :]
        hi = piece(data)
        mid = piece(data - hi)
        pieces = jnp.concatenate([hi, mid, data - hi - mid], axis=0).astype(BF16)
        pick = (slots == rank[device : device + 1]).astype(F32).astype(BF16)
        picked = picked + lax.dot_general(
            pieces, pick, (((1,), (1,)), ((), ())), preferred_element_type=F32
        )
    return picked[0:8] + picked[8:16] + picked[16:24]


def headings(number):
    which = lax.rem(number, 3)
    pick = lambda values: jnp.where(
        which == 0, values[0], jnp.where(which == 1, values[1], values[2])
    )
    return [pick(cosines), pick(sines), jnp.full(number.shape, 0.6, F32)]


def pulls(segment):
    length = jnp.sqrt(segment[0] * segment[0] + segment[1] * segment[1] + segment[2] * segment[2])
    tension = line_stiffness * (length - rest_length) / rest_length
    return [tension / length * part for part in segment]


def own_lines(me, table_ref, line_platform_ref, offset_ref, line_velocity_ref, line_accel_ref):
    lines, segments = offset_ref.shape[1:]
    shape = (lines, segments)
    row_index = lax.broadcasted_iota(jnp.int32, shape, 0)
    node_index = lax.broadcasted_iota(jnp.int32, shape, 1)
    heading = headings(me * lines + row_index)
    depth = (segments - node_index).astype(F32)
    points = [-line_spacing * heading[c] * depth + offset_ref[c] for c in range(3)]
    fair = [jnp.zeros(shape, F32)] * 3
    for line in range(lines):
        owner = lax.bitwise_xor(me, line_platform_ref[line])
        fair = [jnp.where(row_index == line, table_ref[owner, c], fair[c]) for c in range(3)]
    last = node_index == segments - 1
    following = [
        jnp.where(last, fair[c], pltpu.roll(points[c], segments - 1, 1)) for c in range(3)
    ]
    pull = pulls([following[c] - points[c] for c in range(3)])
    for c in range(3):
        previous = jnp.where(node_index == 0, 0.0, pltpu.roll(pull[c], 1, 1))
        gravity = -node_weight if c == 2 else 0.0
        acceleration = pull[c] - previous + gravity - line_damping * line_velocity_ref[c]
        line_accel_ref[c] = jnp.where(node_index == 0, 0.0, acceleration)


def platform_pulls(me, table_ref, misc_ref, lines):
    shape = (misc_ref.shape[0], LANES)
    sender = lax.bitwise_xor(lax.broadcasted_iota(jnp.int32, shape, 0), jnp.full(shape, me))
    number = lax.broadcasted_iota(jnp.int32, shape, 1)
    heading = headings(sender * lines + number)
    ends = [
        table_ref[0, c] - (-line_spacing * heading[c] + misc_ref[:, 9 + c, :]) for c in range(3)
    ]
    ours = jnp.logical_and(number < lines, misc_ref[:, 12, :] == me.astype(F32))
    taken = [jnp.where(ours, part, 0.0) for part in pulls(ends)]
    return [jnp.sum(jnp.sum(t, axis=0, keepdims=True), axis=1, keepdims=True) for t in taken]


def first_kernel(
    me_ref,
    table_ref,
    thrust_ref,
    restoring_ref,
    line_platform_ref,
    misc_ref,
    pos_ref,
    history_ref,
    memory_ref,
    offset_ref,
    line_velocity_ref,
    block_ref,
    target_pos_ref,
    state_ref,
    line_accel_ref,
    sums_ref,
    *scratch,
):
    me = me_ref[0]
    own_count = pos_ref.shape[1]
    nodes = platform_nodes(me, misc_ref)
    current = jnp.concatenate([nodes[c : c + 1] + table_ref[0, c] for c in range(3)], axis=0)
    target_pos_ref[:, 0:own_count] = pos_ref[...]
    target_pos_ref[:, own_count : own_count + LANES] = current
    target_pos_ref[:, own_count + LANES :] = current
    sums_ref[...] = jnp.zeros_like(sums_ref)
    own_lines(me, table_ref, line_platform_ref, offset_ref, line_velocity_ref, line_accel_ref)
    pull = platform_pulls(me, table_ref, misc_ref, offset_ref.shape[1])
    history = jnp.concatenate([history_ref[j] for j in range(6)], axis=0)
    state_ref[0:8, :] = nodes
    for i in range(6):
        product = jnp.sum(memory_ref[i] * history, axis=0, keepdims=True)
        value = -jnp.sum(product, axis=1, keepdims=True) - restoring_ref[i] * table_ref[0, i]
        if i < 3:
            value = value - pull[i]
        state_ref[8 + i : 9 + i, :] = jnp.broadcast_to(value, (1, LANES))
    scales = strength_scales(me, table_ref, thrust_ref)
    pair_sums([block_ref], scales, target_pos_ref, sums_ref, scratch)


def middle_kernel(count, me_ref, table_ref, thrust_ref, target_pos_ref, before_ref, *rest):
    block_refs, (sums_ref, *scratch) = rest[:count], rest[count:]
    sums_ref[...] = before_ref[...]
    scales = strength_scales(me_ref[0], table_ref, thrust_ref)
    pair_sums(block_refs, scales, target_pos_ref, sums_ref, scratch)


def last_kernel(
    count, me_ref, table_ref, thrust_ref, mass_ref, target_pos_ref, before_ref, state_ref, *rest
):
    block_refs, (induced_ref, accel_ref, sums_ref, *scratch) = rest[:count], rest[count:]
    sums_ref[...] = before_ref[...]
    scales = strength_scales(me_ref[0], table_ref, thrust_ref)
    pair_sums(block_refs, scales, target_pos_ref, sums_ref, scratch)
    tiles = sums_ref.shape[0]

    def velocity(tile):
        sums = sums_ref[tile]
        at = target_pos_ref[:, tile * TILE : (tile + 1) * TILE]
        a = [sums[c : c + 1] + sums[c + 3 : c + 4] for c in range(3)]
        b = [sums[c + 6 : c + 7] + sums[c + 9 : c + 10] + sums[c + 12 : c + 13] for c in range(3)]
        x = [at[c : c + 1] for c in range(3)]
        return [
            (a[1] * x[2] - a[2] * x[1] - b[0]) * inverse_four_pi,
            (a[2] * x[0] - a[0] * x[2] - b[1]) * inverse_four_pi,
            (a[0] * x[1] - a[1] * x[0] - b[2]) * inverse_four_pi,
        ]

    for tile in range(tiles - 1):
        induced_ref[:, tile * TILE : (tile + 1) * TILE] = jnp.concatenate(velocity(tile), axis=0)

    wind = [row[:, 0:LANES] for row in velocity(tiles - 1)]
    arm = [state_ref[3 + c : 4 + c, :] for c in range(3)]
    turn = [table_ref[0, 9 + c] for c in range(3)]
    rigid = [
        table_ref[0, 6] + (turn[1] * arm[2] - turn[2] * arm[1]),
        table_ref[0, 7] + (turn[2] * arm[0] - turn[0] * arm[2]),
        table_ref[0, 8] + (turn[0] * arm[1] - turn[1] * arm[0]),
    ]
    relative = [1.0 + wind[0] - rigid[0], wind[1] - rigid[1], wind[2] - rigid[2]]
    magnitude = jnp.sqrt(
        relative[0] * relative[0] + relative[1] * relative[1] + relative[2] * relative[2]
    )
    force = [state_ref[6:7, :] * magnitude * row for row in relative]
    moment = [
        arm[1] * force[2] - arm[2] * force[1],
        arm[2] * force[0] - arm[0] * force[2],
        arm[0] * force[1] - arm[1] * force[0],
    ]
    total = [
        jnp.sum(row, axis=1, keepdims=True) + state_ref[8 + i : 9 + i, 0:1]
        for i, row in enumerate(force + moment)
    ]
    lane = lax.broadcasted_iota(jnp.int32, (1, LANES), 1)
    result = jnp.zeros((1, LANES), F32)
    for i in range(6):
        value = mass_ref[i, 0] * total[0]
        for j in range(1, 6):
            value = value + mass_ref[i, j] * total[j]
        result = jnp.where(lane == i, value, result)
    accel_ref[...] = result[:, 0:6]


def shards(
    particle_pos,
    vorticity,
    particle_owner,
    thrust_coef,
    node_pos,
    lever_arm,
    chord_coef,
    node_platform,
    platform_pos,
    platform_vel,
    velocity_history,
    memory_kernel,
    restoring,
    inverse_mass,
    line_offset,
    line_velocity,
    line_platform,
):
    devices = lax.axis_size("blk")
    me = lax.axis_index("blk")
    own_count = particle_pos.shape[1]
    segments = line_offset.shape[2]
    tiles = own_count // TILE + 1

    def wide(rows):
        return jnp.pad(rows, ((0, 0), (0, LANES - rows.shape[1])))

    motion = jnp.concatenate([platform_pos, platform_vel], axis=0).reshape(1, 12)
    misc = jnp.concatenate(
        [
            node_pos,
            lever_arm,
            chord_coef[None],
            node_platform.astype(F32)[None],
            wide(motion),
            wide(line_offset[:, :, segments - 1]),
            wide(line_platform.astype(F32)[None]),
            jnp.zeros((3, LANES), F32),
        ],
        axis=0,
    )[None]
    own = jnp.concatenate(
        [
            particle_pos,
            vorticity,
            particle_owner.astype(F32)[None],
            jnp.zeros((1, own_count), F32),
        ],
        axis=0,
    )[None]

    def swap(values, distance):
        return lax.ppermute(values, "blk", [(i, i ^ distance) for i in range(devices)])

    distance = 1
    while distance < devices:
        misc = jnp.concatenate([misc, swap(misc, distance)], axis=0)
        distance *= 2
    table = misc[:, 8, 0:16]

    near = [swap(own, 1), swap(own, 2)]
    near.append(swap(near[1], 1))
    direct = []
    if devices > 4:
        direct.append(jnp.concatenate([swap(own, 4), swap(own, 6)], axis=0))

    smem = pl.BlockSpec(memory_space=pltpu.SMEM)
    vmem = pl.BlockSpec(memory_space=pltpu.VMEM)
    sums_shape = jax.ShapeDtypeStruct((tiles, 16, TILE), F32)

    def call(kernel, scalars, arrays, blocks, out_shape):
        count = sum(block.shape[0] for block in blocks)
        rows = count * own_count // QUARTERS
        reach = next(r for r in (1024, 512) if rows % r == 0)
        work = count * own_count * tiles * TILE
        return pl.pallas_call(
            kernel,
            in_specs=[smem] * len(scalars) + [vmem] * (len(arrays) + len(blocks)),
            out_specs=(vmem,) * len(out_shape),
            out_shape=out_shape,
            scratch_shapes=[
                pltpu.VMEM((rows, LANES), BF16),
                pltpu.VMEM((QUARTERS, 16, rows), BF16),
                pltpu.VMEM((tiles * QUARTERS, LANES, TILE), BF16),
                pltpu.VMEM((QUARTERS * reach, TILE), F32),
                pltpu.VMEM((QUARTERS * reach, TILE), F32),
            ],
            compiler_params=pltpu.CompilerParams(vmem_limit_bytes=48 * 2**20),
            cost_estimate=pl.CostEstimate(
                flops=1200 * work, bytes_accessed=count * own_count * 32, transcendentals=0
            ),
            name="pairs",
        )(*scalars, *arrays, *blocks)

    me = me.astype(jnp.int32)[None]
    target_pos, state, line_accel, sums = call(
        first_kernel,
        [me, table, thrust_coef, restoring, line_platform],
        [misc, particle_pos, jnp.transpose(velocity_history, (1, 0, 2)), memory_kernel]
        + [line_offset, line_velocity],
        [own],
        (
            jax.ShapeDtypeStruct((3, tiles * TILE), F32),
            jax.ShapeDtypeStruct((16, LANES), F32),
            jax.ShapeDtypeStruct(line_offset.shape, F32),
            sums_shape,
        ),
    )
    groups = [near]
    distance = 4
    while len(groups) < 2 or distance < devices:
        own, sums, *direct = lax.optimization_barrier((own, sums, *direct))
        if distance < devices:
            groups.append([direct[-1], swap(direct[-1], 1)])
        distance *= 2
        if distance < devices:
            sent = [swap(own, d) for d in range(distance, 2 * distance, 2)]
            direct.append(jnp.concatenate(sent, axis=0))
        if len(groups) < 2:
            break
        blocks = groups.pop(0)
        (sums,) = call(
            functools.partial(middle_kernel, len(blocks)),
            [me, table, thrust_coef],
            [target_pos, sums],
            blocks,
            (sums_shape,),
        )
    blocks = groups[-1]
    induced, accel, unused = call(
        functools.partial(last_kernel, len(blocks)),
        [me, table, thrust_coef, inverse_mass],
        [target_pos, sums, state],
        blocks,
        (
            jax.ShapeDtypeStruct(particle_pos.shape, F32),
            jax.ShapeDtypeStruct((1, 6), F32),
            sums_shape,
        ),
    )
    return (induced, accel.reshape(6, 1), line_accel)


def solution(mesh):
    return jax.shard_map(
        shards,
        mesh=mesh,
        in_specs=(
            P(None, ("farm", "blk")),
            P(None, ("farm", "blk")),
            P(("farm", "blk")),
            P("farm"),
            P(None, ("farm", "blk")),
            P(None, ("farm", "blk")),
            P(("farm", "blk")),
            P(("farm", "blk")),
            P(None, ("farm", "blk")),
            P(None, ("farm", "blk")),
            P(("farm", "blk"), None, None),
            P(),
            P(),
            P(),
            P(None, ("farm", "blk"), None),
            P(None, ("farm", "blk"), None),
            P(("farm", "blk")),
        ),
        out_specs=(
            P(None, ("farm", "blk")),
            P(None, ("farm", "blk")),
            P(None, ("farm", "blk"), None),
        ),
        check_vma=False,
    )
```

time: 134 us -> 128 us (0.955)
  waiting for transfers between devices: 11 us -> 5.06 us
  local copies, waits for them, and re-layouts: 7.28 us -> 1.95 us
  Pallas kernels: 95.3 us -> 98.1 us
  starting transfers between devices: 18.1 us -> 20.2 us
    ppermute x12 -> x15, waiting for transfers between devices: 11 us -> 5.06 us  [swap(): lax.ppermute(values, 'blk', [(i, i ^ distance) for i in range(devices)])]
    unnamed x34 -> x28, local copies, waits for them, and re-layouts: 5.04 us -> 1.55 us
    pallas_call x1 -> x4, Pallas kernels: 95.3 us -> 98.1 us  [call(): pl.pallas_call(kernel, in_specs=[smem] * len(scalars) + [vmem] * (len(arr...]
    ppermute x12 -> x15, starting transfers between devices: 18.1 us -> 20.2 us  [swap(): lax.ppermute(values, 'blk', [(i, i ^ distance) for i in range(devices)])]
  transfers between devices with their start and end apart: 12 -> 15, of which waited for: 4 -> 5; matrix products, arithmetic and copies ran while one was open for 1% -> 0% of each run, Pallas kernels for 0% -> 40%
where the time goes in v2:
time: 128 us
  Pallas kernels  98.1 us (77%)
  starting transfers between devices  20.2 us (16%)
  waiting for transfers between devices  5.06 us (4%)
  local copies, waits for them, and re-layouts  1.95 us (2%)
  other arithmetic  1.6 us (1%)
    pallas_call x4, Pallas kernels, call(): pl.pallas_call(kernel, in_specs=[smem] * len(scalars) + [vmem] * (len(arr...  98.1 us
    ppermute x15, starting transfers between devices, swap(): lax.ppermute(values, 'blk', [(i, i ^ distance) for i in range(devices)])  20.2 us
    ppermute x15, waiting for transfers between devices, swap(): lax.ppermute(values, 'blk', [(i, i ^ distance) for i in range(devices)])  5.06 us
  transfers between devices with their start and end apart: 15, of which 5 were waited for; matrix products, arithmetic and copies ran while one was open for 0% of the time, Pallas kernels for 40%

profile of v2, /device:TPU:0, one launch (start us, length us, event | category | flops | bytes accessed | tf_op | source)
XLA Modules:
  0.0 127.8 jit_solution(16563936871855555667)
XLA Ops:
  0.6 0.0 copy-start.6
  0.6 0.0 copy-start.1
  0.7 0.7 convert_bitcast_fusion.1
  1.3 0.0 copy-done.6
  1.3 0.7 maximum_bitcast_fusion.1
  2.1 0.0 copy-done.1
  2.1 0.2 slice_reduce_fusion
  2.3 0.0 copy-start.11
  2.3 0.0 copy-start.12
  2.3 0.6 copy-done.13
  2.9 0.0 copy-done.11
  3.0 0.0 copy-done.12
  3.0 0.5 collective-permute-start
  3.5 0.8 collective-permute-done
  4.4 2.9 %collective-permute-start.1 = (f32[2,16,128]{2,0,1:T(2,128)S(1)}, f32[2,16,128]{2,0,1:T(2,128)S(1)}, u32[]{:S(2)}, u32[]{:S(2)}) collective-permute-start(f32[2,16,128]{2,0,1:T(2,128)S(1)} %pad_maximum_fusion.4), channel_id=1, source_target_pairs={{0,2},{1,3},{2,0},{3,1},{4,6},{5,7},{6,4},{7,5},{8,10},{9,11},{10,... | collective-permute-start | bytes 49160 | tf_op jit(solution)/shard_map/ppermute | solution.py:422
  7.3 0.0 copy-done.10
  7.3 0.1 pad.24.clone
  7.4 1.6 %collective-permute-done.1 = f32[2,16,128]{2,0,1:T(2,128)S(1)} collective-permute-done((f32[2,16,128]{2,0,1:T(2,128)S(1)}, f32[2,16,128]{2,0,1:T(2,128)S(1)}, u32[]{:S(2)}, u32[]{:S(2)}) %collective-permute-start.1) | collective-permute-done | bytes 16416 | tf_op jit(solution)/shard_map/ppermute | solution.py:422
  9.1 2.1 %collective-permute-start.2 = (f32[4,16,128]{2,0,1:T(4,128)S(1)}, f32[4,16,128]{2,0,1:T(4,128)S(1)}, u32[]{:S(2)}, u32[]{:S(2)}) collective-permute-start(f32[4,16,128]{2,0,1:T(4,128)S(1)} %pad_maximum_fusion.3), channel_id=1, source_target_pairs={{0,4},{1,5},{2,6},{3,7},{4,0},{5,1},{6,2},{7,3},{8,12},{9,13},{10,... | collective-permute-start | bytes 98312 | tf_op jit(solution)/shard_map/ppermute | solution.py:422
  11.2 0.0 copy-done
  11.2 0.0 copy-done.9
  11.2 0.1 maximum_bitcast_fusion.block_ref
  11.3 1.5 %collective-permute-start.7 = (f32[1,8,2048]{2,1,0:T(8,128)S(1)}, f32[1,8,2048]{2,1,0:T(8,128)S(1)}, u32[]{:S(2)}, u32[]{:S(2)}) collective-permute-start(f32[1,8,2048]{2,1,0:T(8,128)S(1)} %maximum_bitcast_fusion.block_ref), channel_id=1, source_target_pairs={{0,2},{1,3},{2,0},{3,1},{4,6},{5,7},{6,4},{7,5},{8,10},{9,11},{10,... | collective-permute-start | bytes 196616 | tf_op jit(solution)/shard_map/ppermute | solution.py:422
  12.8 0.0 collective-permute-start.6
  12.8 0.0 collective-permute-start.5
  12.9 1.9 %collective-permute-start.4 = (f32[1,8,2048]{2,1,0:T(8,128)S(1)}, f32[1,8,2048]{2,1,0:T(8,128)S(1)}, u32[]{:S(2)}, u32[]{:S(2)}) collective-permute-start(f32[1,8,2048]{2,1,0:T(8,128)S(1)} %maximum_bitcast_fusion.block_ref), channel_id=1, source_target_pairs={{0,4},{1,5},{2,6},{3,7},{4,0},{5,1},{6,2},{7,3},{8,12},{9,13},{10,... | collective-permute-start | bytes 196616 | tf_op jit(solution)/shard_map/ppermute | solution.py:422
  14.8 0.0 collective-permute-done.2
  14.8 2.7 %collective-permute-start.3 = (f32[8,16,128]{2,0,1:T(8,128)S(1)}, f32[8,16,128]{2,0,1:T(8,128)S(1)}, u32[]{:S(2)}, u32[]{:S(2)}) collective-permute-start(f32[8,16,128]{2,0,1:T(8,128)S(1)} %pad_maximum_fusion.2), channel_id=1, source_target_pairs={{0,8},{1,9},{2,10},{3,11},{4,12},{5,13},{6,14},{7,15},{8,0},{9,1},... | collective-permute-start | bytes 196616 | tf_op jit(solution)/shard_map/ppermute | solution.py:422
  17.5 0.0 collective-permute-done.7.rest_1_
  17.5 0.0 collective-permute-start.8
  17.5 1.1 collective-permute-done.5
  18.6 0.9 collective-permute-done.4
  19.5 0.6 collective-permute-done.3
  20.1 0.1 concatenate.35
  20.1 0.0 copy-start.2
  20.2 0.0 copy-start.3
  20.2 0.0 copy-start.4
  20.2 0.0 copy-start.7
  20.3 0.0 copy-start.8
  20.3 0.8 copy-done.2
  21.1 0.0 copy-done.3
  21.1 0.0 copy-done.4
  21.1 0.0 copy-done.7
  21.1 0.0 copy-done.8
  21.1 7.9 %pairs.4 = (f32[3,2304]{1,0:T(4,128)S(1)}, f32[16,128]{1,0:T(8,128)S(1)}, f32[3,3,128]{2,1,0:T(4,128)}, f32[9,16,256]{2,1,0:T(8,128)S(1)}) custom-call(s32[1]{0:T(128)} %bitcast.me_ref, f32[16,16]{1,0:T(8,128)S(1)} %slice_bitcast_fusion.table_ref, f32[16]{0:T(128)S(1)} %copy-done.8, f32[6]{0:T(128)S(1)} %copy-done.7, s32[3]{0:T(128)S(1)} %copy-done.6, ...), custom_call_target="tpu_custom_call" | custom-call | flops 5662310400 | bytes 65536 | tf_op jit(solution)/shard_map/pairs/pallas_call | solution.py:445
  29.0 4.9 %collective-permute-start.12 = (f32[1,8,2048]{2,1,0:T(8,128)S(1)}, f32[1,8,2048]{2,1,0:T(8,128)S(1)}, u32[]{:S(2)}, u32[]{:S(2)}) collective-permute-start(f32[1,8,2048]{2,1,0:T(8,128)S(1)} %maximum_bitcast_fusion.block_ref), channel_id=1, source_target_pairs={{0,14},{1,15},{2,12},{3,13},{4,10},{5,11},{6,8},{7,9},{8,6},{9,7},... | collective-permute-start | bytes 196616 | tf_op jit(solution)/shard_map/ppermute | solution.py:422
  33.9 0.0 collective-permute-start.11
  33.9 0.7 collective-permute-start.10
  34.6 0.0 collective-permute-done.6.rest_0_
  34.6 2.3 %collective-permute-start.9 = (f32[1,8,2048]{2,1,0:T(8,128)S(1)}, f32[1,8,2048]{2,1,0:T(8,128)S(1)}, u32[]{:S(2)}, u32[]{:S(2)}) collective-permute-start(f32[1,8,2048]{2,1,0:T(8,128)S(1)} %maximum_bitcast_fusion.block_ref), channel_id=1, source_target_pairs={{0,8},{1,9},{2,10},{3,11},{4,12},{5,13},{6,14},{7,15},{8,0},{9,1},... | collective-permute-start | bytes 196616 | tf_op jit(solution)/shard_map/ppermute | solution.py:422
  36.9 0.0 collective-permute-done.8.rest_2_
  36.9 0.0 collective-permute-start.13
  36.9 19.3 %pairs.5.before_ref = f32[9,16,256]{2,1,0:T(8,128)S(1)} custom-call(s32[1]{0:T(128)} %bitcast.me_ref, f32[16,16]{1,0:T(8,128)S(1)} %slice_bitcast_fusion.table_ref, f32[16]{0:T(128)S(1)} %copy-done.8, f32[3,2304]{1,0:T(4,128)S(1)} %get-tuple-element.15.target_pos_ref, f32[9,16,256]{2,1,0:T(8,128)S(1)} %get-tuple-element.18.before_ref, ...), custom_call_target="tpu_custom_call" | custom-call | flops 16986931200 | bytes 196608 | tf_op jit(solution)/shard_map/pairs/pallas_call | solution.py:445
  56.2 0.0 collective-permute-done.12
  56.2 0.0 collective-permute-done.11
  56.2 0.0 collective-permute-done.10
  56.2 0.0 collective-permute-done.9
  56.2 0.0 copy-start.5
  56.3 0.6 collective-permute-start.14
  56.8 0.0 collective-permute-done.13.rest_1_
  56.8 23.7 %pairs.6.before_ref = f32[9,16,256]{2,1,0:T(8,128)S(1)} custom-call(s32[1]{0:T(128)} %bitcast.me_ref, f32[16,16]{1,0:T(8,128)S(1)} %slice_bitcast_fusion.table_ref, f32[16]{0:T(128)S(1)} %copy-done.8, f32[3,2304]{1,0:T(4,128)S(1)} %get-tuple-element.15.target_pos_ref, f32[9,16,256]{2,1,0:T(8,128)S(1)} %pairs.5.before_ref, ...), custom_call_target="tpu_custom_call" | custom-call | flops 22649241600 | bytes 262144 | tf_op jit(solution)/shard_map/pairs/pallas_call | solution.py:445
  80.5 0.0 collective-permute-done.14.rest_1_
  80.5 0.0 copy-done.5
  80.5 47.3 %pairs.7 = (f32[3,2048]{1,0:T(4,128)}, f32[1,6]{1,0:T(1,128)}, f32[9,16,256]{2,1,0:T(8,128)}) custom-call(s32[1]{0:T(128)} %bitcast.me_ref, f32[16,16]{1,0:T(8,128)S(1)} %slice_bitcast_fusion.table_ref, f32[16]{0:T(128)S(1)} %copy-done.8, f32[6,6]{1,0:T(8,128)S(1)} %copy-done.5, f32[3,2304]{1,0:T(4,128)S(1)} %get-tuple-element.15.target_pos_ref, ...), custom_call_target="tpu_custom_call" | custom-call | flops 45298483200 | bytes 524288 | tf_op jit(solution)/shard_map/pairs/pallas_call | solution.py:445
  (18 shorter events, 0.2 us)
Async XLA Ops:
  0.6 0.7 copy-start.6
  0.6 1.4 %copy-start.1 = (f32[3,3,128]{2,1,0:T(4,128)S(1)}, f32[3,3,128]{2,1,0:T(4,128)}, u32[]{:S(2)}) copy-start(f32[3,3,128]{2,1,0:T(4,128)} %offset_ref.1) | copy-start | bytes 13828
  2.3 0.7 copy-start.13
  2.3 0.7 copy-start.11
  2.3 0.7 copy-start.12
  3.0 4.3 %copy-start.10 = (s32[2048]{0:T(1024)S(1)}, s32[2048]{0:T(1024)}, u32[]{:S(2)}) copy-start(s32[2048]{0:T(1024)} %param.19) | copy-start | bytes 24580
  3.0 1.3 %collective-permute-start = (f32[1,16,128]{2,0,1:T(1,128)S(1)}, f32[1,16,128]{2,0,1:T(1,128)S(1)}, u32[]{:S(2)}, u32[]{:S(2)}) collective-permute-start(f32[1,16,128]{2,0,1:T(1,128)S(1)} %bitcast.18), channel_id=1, source_target_pairs={{0,1},{1,0},{2,3},{3,2},{4,5},{5,4},{6,7},{7,6},{8,9},{9,8},{10,11... | collective-permute-start | bytes 24584 | tf_op jit(solution)/shard_map/ppermute | solution.py:422
  4.4 4.6 %collective-permute-start.1 = (f32[2,16,128]{2,0,1:T(2,128)S(1)}, f32[2,16,128]{2,0,1:T(2,128)S(1)}, u32[]{:S(2)}, u32[]{:S(2)}) collective-permute-start(f32[2,16,128]{2,0,1:T(2,128)S(1)} %pad_maximum_fusion.4), channel_id=1, source_target_pairs={{0,2},{1,3},{2,0},{3,1},{4,6},{5,7},{6,4},{7,5},{8,10},{9,11},{10,... | collective-permute-start | bytes 49160 | tf_op jit(solution)/shard_map/ppermute | solution.py:422
  7.4 3.8 %copy-start = (f32[3,2048]{1,0:T(4,128)S(1)}, f32[3,2048]{1,0:T(4,128)}, u32[]{:S(2)}) copy-start(f32[3,2048]{1,0:T(4,128)} %pos_ref.1) | copy-start | bytes 73732
  7.4 3.8 %copy-start.9 = (f32[3,2048]{1,0:T(4,128)S(1)}, f32[3,2048]{1,0:T(4,128)}, u32[]{:S(2)}) copy-start(f32[3,2048]{1,0:T(4,128)} %param.18) | copy-start | bytes 73732
  9.1 5.7 %collective-permute-start.2 = (f32[4,16,128]{2,0,1:T(4,128)S(1)}, f32[4,16,128]{2,0,1:T(4,128)S(1)}, u32[]{:S(2)}, u32[]{:S(2)}) collective-permute-start(f32[4,16,128]{2,0,1:T(4,128)S(1)} %pad_maximum_fusion.3), channel_id=1, source_target_pairs={{0,4},{1,5},{2,6},{3,7},{4,0},{5,1},{6,2},{7,3},{8,12},{9,13},{10,... | collective-permute-start | bytes 98312 | tf_op jit(solution)/shard_map/ppermute | solution.py:422
  11.3 6.2 %collective-permute-start.7 = (f32[1,8,2048]{2,1,0:T(8,128)S(1)}, f32[1,8,2048]{2,1,0:T(8,128)S(1)}, u32[]{:S(2)}, u32[]{:S(2)}) collective-permute-start(f32[1,8,2048]{2,1,0:T(8,128)S(1)} %maximum_bitcast_fusion.block_ref), channel_id=1, source_target_pairs={{0,2},{1,3},{2,0},{3,1},{4,6},{5,7},{6,4},{7,5},{8,10},{9,11},{10,... | collective-permute-start | bytes 196616 | tf_op jit(solution)/shard_map/ppermute | solution.py:422
  12.8 21.7 %collective-permute-start.6 = (f32[1,8,2048]{2,1,0:T(8,128)S(1)}, f32[1,8,2048]{2,1,0:T(8,128)S(1)}, u32[]{:S(2)}, u32[]{:S(2)}) collective-permute-start(f32[1,8,2048]{2,1,0:T(8,128)S(1)} %maximum_bitcast_fusion.block_ref), channel_id=1, source_target_pairs={{0,1},{1,0},{2,3},{3,2},{4,5},{5,4},{6,7},{7,6},{8,9},{9,8},{10,11... | collective-permute-start | bytes 196616 | tf_op jit(solution)/shard_map/ppermute | solution.py:422
  12.8 5.8 %collective-permute-start.5 = (f32[1,8,2048]{2,1,0:T(8,128)S(1)}, f32[1,8,2048]{2,1,0:T(8,128)S(1)}, u32[]{:S(2)}, u32[]{:S(2)}) collective-permute-start(f32[1,8,2048]{2,1,0:T(8,128)S(1)} %maximum_bitcast_fusion.block_ref), channel_id=1, source_target_pairs={{0,6},{1,7},{2,4},{3,5},{4,2},{5,3},{6,0},{7,1},{8,14},{9,15},{10,... | collective-permute-start | bytes 196616 | tf_op jit(solution)/shard_map/ppermute | solution.py:422
  12.9 6.6 %collective-permute-start.4 = (f32[1,8,2048]{2,1,0:T(8,128)S(1)}, f32[1,8,2048]{2,1,0:T(8,128)S(1)}, u32[]{:S(2)}, u32[]{:S(2)}) collective-permute-start(f32[1,8,2048]{2,1,0:T(8,128)S(1)} %maximum_bitcast_fusion.block_ref), channel_id=1, source_target_pairs={{0,4},{1,5},{2,6},{3,7},{4,0},{5,1},{6,2},{7,3},{8,12},{9,13},{10,... | collective-permute-start | bytes 196616 | tf_op jit(solution)/shard_map/ppermute | solution.py:422
  14.8 5.2 %collective-permute-start.3 = (f32[8,16,128]{2,0,1:T(8,128)S(1)}, f32[8,16,128]{2,0,1:T(8,128)S(1)}, u32[]{:S(2)}, u32[]{:S(2)}) collective-permute-start(f32[8,16,128]{2,0,1:T(8,128)S(1)} %pad_maximum_fusion.2), channel_id=1, source_target_pairs={{0,8},{1,9},{2,10},{3,11},{4,12},{5,13},{6,14},{7,15},{8,0},{9,1},... | collective-permute-start | bytes 196616 | tf_op jit(solution)/shard_map/ppermute | solution.py:422
  17.5 19.4 %collective-permute-start.8 = (f32[1,8,2048]{2,1,0:T(8,128)S(1)}, f32[1,8,2048]{2,1,0:T(8,128)S(1)}, u32[]{:S(2)}, u32[]{:S(2)}) collective-permute-start(f32[1,8,2048]{2,1,0:T(8,128)S(1)} %collective-permute-done.7.rest_1_), channel_id=1, source_target_pairs={{0,1},{1,0},{2,3},{3,2},{4,5},{5,4},{6,7},{7,6},{8,9},{9,8},{10,11... | collective-permute-start | bytes 196616 | tf_op jit(solution)/shard_map/ppermute | solution.py:422
  20.1 0.9 copy-start.2
  20.2 0.9 copy-start.3
  20.2 0.9 copy-start.4
  20.2 0.8 copy-start.7
  20.3 0.8 copy-start.8
  29.0 27.2 %collective-permute-start.12 = (f32[1,8,2048]{2,1,0:T(8,128)S(1)}, f32[1,8,2048]{2,1,0:T(8,128)S(1)}, u32[]{:S(2)}, u32[]{:S(2)}) collective-permute-start(f32[1,8,2048]{2,1,0:T(8,128)S(1)} %maximum_bitcast_fusion.block_ref), channel_id=1, source_target_pairs={{0,14},{1,15},{2,12},{3,13},{4,10},{5,11},{6,8},{7,9},{8,6},{9,7},... | collective-permute-start | bytes 196616 | tf_op jit(solution)/shard_map/ppermute | solution.py:422
  33.9 22.3 %collective-permute-start.11 = (f32[1,8,2048]{2,1,0:T(8,128)S(1)}, f32[1,8,2048]{2,1,0:T(8,128)S(1)}, u32[]{:S(2)}, u32[]{:S(2)}) collective-permute-start(f32[1,8,2048]{2,1,0:T(8,128)S(1)} %maximum_bitcast_fusion.block_ref), channel_id=1, source_target_pairs={{0,12},{1,13},{2,14},{3,15},{4,8},{5,9},{6,10},{7,11},{8,4},{9,5},... | collective-permute-start | bytes 196616 | tf_op jit(solution)/shard_map/ppermute | solution.py:422
  33.9 22.3 %collective-permute-start.10 = (f32[1,8,2048]{2,1,0:T(8,128)S(1)}, f32[1,8,2048]{2,1,0:T(8,128)S(1)}, u32[]{:S(2)}, u32[]{:S(2)}) collective-permute-start(f32[1,8,2048]{2,1,0:T(8,128)S(1)} %maximum_bitcast_fusion.block_ref), channel_id=1, source_target_pairs={{0,10},{1,11},{2,8},{3,9},{4,14},{5,15},{6,12},{7,13},{8,2},{9,3},... | collective-permute-start | bytes 196616 | tf_op jit(solution)/shard_map/ppermute | solution.py:422
  34.6 21.6 %collective-permute-start.9 = (f32[1,8,2048]{2,1,0:T(8,128)S(1)}, f32[1,8,2048]{2,1,0:T(8,128)S(1)}, u32[]{:S(2)}, u32[]{:S(2)}) collective-permute-start(f32[1,8,2048]{2,1,0:T(8,128)S(1)} %maximum_bitcast_fusion.block_ref), channel_id=1, source_target_pairs={{0,8},{1,9},{2,10},{3,11},{4,12},{5,13},{6,14},{7,15},{8,0},{9,1},... | collective-permute-start | bytes 196616 | tf_op jit(solution)/shard_map/ppermute | solution.py:422
  36.9 19.9 %collective-permute-start.13 = (f32[2,8,2048]{2,1,0:T(8,128)S(1)}, f32[2,8,2048]{2,1,0:T(8,128)S(1)}, u32[]{:S(2)}, u32[]{:S(2)}) collective-permute-start(f32[2,8,2048]{2,1,0:T(8,128)S(1)} %pad_maximum_fusion.1.rest_0_), channel_id=1, source_target_pairs={{0,1},{1,0},{2,3},{3,2},{4,5},{5,4},{6,7},{7,6},{8,9},{9,8},{10,11... | collective-permute-start | bytes 393224 | tf_op jit(solution)/shard_map/ppermute | solution.py:422
  56.2 24.3 %copy-start.5 = (f32[6,6]{1,0:T(8,128)S(1)}, f32[6,6]{1,0:T(8,128)}, u32[]{:S(2)}) copy-start(f32[6,6]{1,0:T(8,128)} %mass_ref.1) | copy-start | bytes 436
  56.3 24.2 %collective-permute-start.14 = (f32[4,8,2048]{2,1,0:T(8,128)S(1)}, f32[4,8,2048]{2,1,0:T(8,128)S(1)}, u32[]{:S(2)}, u32[]{:S(2)}) collective-permute-start(f32[4,8,2048]{2,1,0:T(8,128)S(1)} %pad_maximum_fusion.rest_0_), channel_id=1, source_target_pairs={{0,1},{1,0},{2,3},{3,2},{4,5},{5,4},{6,7},{7,6},{8,9},{9,8},{10,11... | collective-permute-start | bytes 786440 | tf_op jit(solution)/shard_map/ppermute | solution.py:422

commit v3 on v2

--- a/solution.py
+++ b/solution.py
@@ -102,13 +102,22 @@
 def pair_sums(block_refs, scales, target_pos_ref, sums_ref, scratch):
     rows_ref, weights_ref, targets_ref, even_ref, odd_ref = scratch
     quarter = block_refs[0].shape[2] // QUARTERS
-    tiles = sums_ref.shape[0]
+    tiles = sums_ref.shape[0] - 1
+    halves = QUARTERS // 2
     for tile in range(tiles):
         features = target_rows(target_pos_ref[:, tile * TILE : (tile + 1) * TILE]).astype(BF16)
         for part in range(QUARTERS):
             slot = targets_ref.at[tile * QUARTERS + part]
             slot[...] = jnp.zeros((LANES, TILE), BF16)
             slot[part * FEATURES : (part + 1) * FEATURES, :] = features
+    features = target_rows(target_pos_ref[:, tiles * TILE : (tiles + 1) * TILE]).astype(BF16)
+    left = features[:, 0:LANES]
+    for half in range(halves):
+        slot = targets_ref.at[tiles * QUARTERS + half]
+        slot[...] = jnp.zeros((LANES, TILE), BF16)
+        for side in range(2):
+            part = 2 * half + side
+            slot[part * FEATURES : (part + 1) * FEATURES, side * LANES : (side + 1) * LANES] = left
 
     first = 0
     for block_ref in block_refs:
@@ -129,24 +138,36 @@
                 ]
             return carry
 
-        lax.fori_loop(0, block_ref.shape[0], prepare, 0)
+        lax.fori_loop(0, block_ref.shape[0], prepare, 0, unroll=4)
         first += block_ref.shape[0]
 
+    rows = rows_ref.shape[0]
     reach = even_ref.shape[0] // QUARTERS
-    chunks = rows_ref.shape[0] // reach
+    chunks = rows // reach
     steps = tiles * chunks
-    span = min(SPAN, reach)
+    span = SPAN
+
+    def distances_into(buffer, at, start, count, features):
+        for k in range(0, count, span):
+            buffer[at + k : at + k + span, :] = jnp.dot(
+                rows_ref[pl.ds(start + k, span), :], features, preferred_element_type=F32
+            )
+
+    def summed(buffer, at, weights):
+        root = lax.rsqrt(buffer[at : at + span, :])
+        pair = root * root * root
+        high = pair.astype(BF16)
+        low = (pair - high.astype(F32)).astype(BF16)
+        return jnp.dot(weights, high, preferred_element_type=F32) + jnp.dot(
+            weights, low, preferred_element_type=F32
+        )
 
     def distances(step, buffer):
         tile = step // chunks
         start = pl.multiple_of(step % chunks * reach, reach)
         for part in range(QUARTERS):
             features = targets_ref[tile * QUARTERS + part]
-            for k in range(0, reach, span):
-                at = part * reach + k
-                buffer[at : at + span, :] = jnp.dot(
-                    rows_ref[pl.ds(start + k, span), :], features, preferred_element_type=F32
-                )
+            distances_into(buffer, part * reach, start, reach, features)
 
     def add_up(step, buffer):
         tile = step // chunks
@@ -154,15 +175,25 @@
         total = jnp.zeros((16, TILE), F32)
         for part in range(QUARTERS):
             for k in range(0, reach, span):
-                at = part * reach + k
-                root = lax.rsqrt(buffer[at : at + span, :])
-                pair = root * root * root
-                high = pair.astype(BF16)
-                low = (pair - high.astype(F32)).astype(BF16)
                 weights = weights_ref[part, :, pl.ds(start + k, span)]
-                total = total + jnp.dot(weights, high, preferred_element_type=F32)
-                total = total + jnp.dot(weights, low, preferred_element_type=F32)
+                total = total + summed(buffer, part * reach + k, weights)
         sums_ref[tile] += total
+
+    node_reach = min(rows, 2 * reach)
+
+    def node_distances(start, buffer):
+        for half in range(halves):
+            features = targets_ref[tiles * QUARTERS + half]
+            distances_into(buffer, half * node_reach, start, node_reach, features)
+
+    def node_add_up(start, buffer):
+        total = jnp.zeros((32, TILE), F32)
+        for half in range(halves):
+            for k in range(0, node_reach, span):
+                weights = weights_ref[2 * half : 2 * half + 2, :, pl.ds(start + k, span)]
+                weights = weights.reshape(32, span)
+                total = total + summed(buffer, half * node_reach + k, weights)
+        sums_ref[tiles, :, 0:LANES] += total[0:16, 0:LANES] + total[16:32, LANES:]
 
     def two_steps(index, carry):
         step = 2 * index
@@ -175,17 +206,64 @@
     distances(0, even_ref)
     doubles = (steps - 1) // 2
     lax.fori_loop(0, doubles, two_steps, 0)
-    if steps % 2 == 0:
-        distances(steps - 1, odd_ref)
-        add_up(steps - 2, even_ref)
-        add_up(steps - 1, odd_ref)
-    else:
-        add_up(steps - 1, even_ref)
+    stages = [(functools.partial(distances, k), functools.partial(add_up, k)) for k in range(2 * doubles, steps)]
+    stages += [
+        (functools.partial(node_distances, start), functools.partial(node_add_up, start))
+        for start in range(0, rows, node_reach)
+    ]
+    buffers = [even_ref, odd_ref]
+    for index, (unused, add) in enumerate(stages):
+        if index + 1 < len(stages):
+            stages[index + 1][0](buffers[(index + 1) % 2])
+        add(buffers[index % 2])
+
+
+def misc_row(misc_ref, row):
+    return misc_ref[:, row * LANES : (row + 1) * LANES]
+
+
+def pack_kernel(
+    line_platform_ref,
+    pos_ref,
+    vorticity_ref,
+    owner_ref,
+    node_pos_ref,
+    lever_arm_ref,
+    chord_ref,
+    node_platform_ref,
+    platform_pos_ref,
+    platform_vel_ref,
+    offset_ref,
+    own_ref,
+):
+    own_ref[0, 0:3, :] = pos_ref[...]
+    own_ref[0, 3:6, :] = vorticity_ref[...]
+    own_ref[0, 6:7, :] = owner_ref[...].astype(F32)
+    own_ref[0, 7:8, :] = jnp.zeros(owner_ref.shape, F32)
+
+    def put(row, values):
+        own_ref[0, 7:8, row * LANES : row * LANES + values.shape[1]] = values
+
+    lane = lax.broadcasted_iota(jnp.int32, (1, LANES), 1)
+    for c in range(3):
+        put(c, node_pos_ref[c : c + 1, :])
+        put(3 + c, lever_arm_ref[c : c + 1, :])
+        row = jnp.zeros((1, LANES), F32)
+        for line in range(offset_ref.shape[1]):
+            row = jnp.where(lane == line, offset_ref[c, line : line + 1, LANES - 1 :], row)
+        put(9 + c, row)
+    put(6, chord_ref[...])
+    put(7, node_platform_ref[...].astype(F32))
+    put(8, jnp.concatenate([platform_pos_ref[...], platform_vel_ref[...]], axis=1))
+    row = jnp.zeros((1, LANES), F32)
+    for line in range(offset_ref.shape[1]):
+        row = jnp.where(lane == line, line_platform_ref[line].astype(F32), row)
+    put(12, row)
 
 
 def platform_nodes(me, misc_ref):
     devices = misc_ref.shape[0]
-    on_platform = misc_ref[:, 7, :] == me.astype(F32)
+    on_platform = misc_row(misc_ref, 7) == me.astype(F32)
     mark = on_platform.astype(F32)
     upper = lax.broadcasted_iota(jnp.int32, (LANES, LANES), 0) <= lax.broadcasted_iota(
         jnp.int32, (LANES, LANES), 1
@@ -200,7 +278,9 @@
     slots = lax.broadcasted_iota(jnp.int32, (LANES, LANES), 0).astype(F32)
     picked = jnp.zeros((24, LANES), F32)
     for device in range(devices):
-        data = misc_ref[device, 0:8, :]
+        data = jnp.concatenate(
+            [misc_ref[device : device + 1, k * LANES : (k + 1) * LANES] for k in range(8)], axis=0
+        )
         hi = piece(data)
         mid = piece(data - hi)
         pieces = jnp.concatenate([hi, mid, data - hi - mid], axis=0).astype(BF16)
@@ -255,9 +335,9 @@
     number = lax.broadcasted_iota(jnp.int32, shape, 1)
     heading = headings(sender * lines + number)
     ends = [
-        table_ref[0, c] - (-line_spacing * heading[c] + misc_ref[:, 9 + c, :]) for c in range(3)
+        table_ref[0, c] - (-line_spacing * heading[c] + misc_row(misc_ref, 9 + c)) for c in range(3)
     ]
-    ours = jnp.logical_and(number < lines, misc_ref[:, 12, :] == me.astype(F32))
+    ours = jnp.logical_and(number < lines, misc_row(misc_ref, 12) == me.astype(F32))
     taken = [jnp.where(ours, part, 0.0) for part in pulls(ends)]
     return [jnp.sum(jnp.sum(t, axis=0, keepdims=True), axis=1, keepdims=True) for t in taken]
 
@@ -274,7 +354,7 @@
     memory_ref,
     offset_ref,
     line_velocity_ref,
-    block_ref,
+    base_ref,
     target_pos_ref,
     state_ref,
     line_accel_ref,
@@ -300,7 +380,7 @@
             value = value - pull[i]
         state_ref[8 + i : 9 + i, :] = jnp.broadcast_to(value, (1, LANES))
     scales = strength_scales(me, table_ref, thrust_ref)
-    pair_sums([block_ref], scales, target_pos_ref, sums_ref, scratch)
+    pair_sums([base_ref], scales, target_pos_ref, sums_ref, scratch)
 
 
 def middle_kernel(count, me_ref, table_ref, thrust_ref, target_pos_ref, before_ref, *rest):
@@ -388,60 +468,51 @@
     devices = lax.axis_size("blk")
     me = lax.axis_index("blk")
     own_count = particle_pos.shape[1]
-    segments = line_offset.shape[2]
     tiles = own_count // TILE + 1
 
-    def wide(rows):
-        return jnp.pad(rows, ((0, 0), (0, LANES - rows.shape[1])))
-
-    motion = jnp.concatenate([platform_pos, platform_vel], axis=0).reshape(1, 12)
-    misc = jnp.concatenate(
-        [
-            node_pos,
-            lever_arm,
-            chord_coef[None],
-            node_platform.astype(F32)[None],
-            wide(motion),
-            wide(line_offset[:, :, segments - 1]),
-            wide(line_platform.astype(F32)[None]),
-            jnp.zeros((3, LANES), F32),
-        ],
-        axis=0,
-    )[None]
-    own = jnp.concatenate(
-        [
-            particle_pos,
-            vorticity,
-            particle_owner.astype(F32)[None],
-            jnp.zeros((1, own_count), F32),
-        ],
-        axis=0,
-    )[None]
+    smem = pl.BlockSpec(memory_space=pltpu.SMEM)
+    vmem = pl.BlockSpec(memory_space=pltpu.VMEM)
+    own = pl.pallas_call(
+        pack_kernel,
+        in_specs=[smem] + [vmem] * 10,
+        out_specs=vmem,
+        out_shape=jax.ShapeDtypeStruct((1, 8, own_count), F32),
+        name="pack",
+    )(
+        line_platform,
+        particle_pos,
+        vorticity,
+        particle_owner[None],
+        node_pos,
+        lever_arm,
+        chord_coef[None],
+        node_platform[None],
+        platform_pos.T,
+        platform_vel.T,
+        line_offset,
+    )
 
     def swap(values, distance):
         return lax.ppermute(values, "blk", [(i, i ^ distance) for i in range(devices)])
 
-    distance = 1
+    base = jnp.concatenate([own, swap(own, 1)], axis=0)
+    base = jnp.concatenate([base, swap(base, 2)], axis=0)
+    misc = base[:, 7, :]
+    distance = 4
     while distance < devices:
         misc = jnp.concatenate([misc, swap(misc, distance)], axis=0)
         distance *= 2
-    table = misc[:, 8, 0:16]
-
-    near = [swap(own, 1), swap(own, 2)]
-    near.append(swap(near[1], 1))
-    direct = []
-    if devices > 4:
-        direct.append(jnp.concatenate([swap(own, 4), swap(own, 6)], axis=0))
-
-    smem = pl.BlockSpec(memory_space=pltpu.SMEM)
-    vmem = pl.BlockSpec(memory_space=pltpu.VMEM)
+    misc, base = lax.optimization_barrier((misc, base))
+    far = swap(base, 4)
+    table = misc[:, 8 * LANES : 8 * LANES + 16]
+
     sums_shape = jax.ShapeDtypeStruct((tiles, 16, TILE), F32)
 
     def call(kernel, scalars, arrays, blocks, out_shape):
         count = sum(block.shape[0] for block in blocks)
         rows = count * own_count // QUARTERS
         reach = next(r for r in (1024, 512) if rows % r == 0)
-        work = count * own_count * tiles * TILE
+        work = count * own_count * (tiles * TILE - LANES)
         return pl.pallas_call(
             kernel,
             in_specs=[smem] * len(scalars) + [vmem] * (len(arrays) + len(blocks)),
@@ -467,7 +538,7 @@
         [me, table, thrust_coef, restoring, line_platform],
         [misc, particle_pos, jnp.transpose(velocity_history, (1, 0, 2)), memory_kernel]
         + [line_offset, line_velocity],
-        [own],
+        [base],
         (
             jax.ShapeDtypeStruct((3, tiles * TILE), F32),
             jax.ShapeDtypeStruct((16, LANES), F32),
@@ -475,32 +546,24 @@
             sums_shape,
         ),
     )
-    groups = [near]
-    distance = 4
-    while len(groups) < 2 or distance < devices:
-        own, sums, *direct = lax.optimization_barrier((own, sums, *direct))
-        if distance < devices:
-            groups.append([direct[-1], swap(direct[-1], 1)])
-        distance *= 2
-        if distance < devices:
-            sent = [swap(own, d) for d in range(distance, 2 * distance, 2)]
-            direct.append(jnp.concatenate(sent, axis=0))
-        if len(groups) < 2:
-            break
-        blocks = groups.pop(0)
+    distance = 8
+    while distance < devices:
+        sums, base, far = lax.optimization_barrier((sums, base, far))
+        base = jnp.concatenate([base, far], axis=0)
+        blocks, far = far, swap(base, distance)
         (sums,) = call(
-            functools.partial(middle_kernel, len(blocks)),
+            functools.partial(middle_kernel, 1),
             [me, table, thrust_coef],
             [target_pos, sums],
-            blocks,
+            [blocks],
             (sums_shape,),
         )
-    blocks = groups[-1]
+        distance *= 2
     induced, accel, unused = call(
-        functools.partial(last_kernel, len(blocks)),
+        functools.partial(last_kernel, 1),
         [me, table, thrust_coef, inverse_mass],
         [target_pos, sums, state],
-        blocks,
+        [far],
         (
             jax.ShapeDtypeStruct(particle_pos.shape, F32),
             jax.ShapeDtypeStruct((1, 6), F32),

time: 128 us -> 117 us (0.914)
  starting transfers between devices: 20.2 us -> 13.2 us
  Pallas kernels: 98.1 us -> 91.7 us
  waiting for transfers between devices: 5.06 us -> 9.41 us
    pallas_call x4 -> x3, Pallas kernels: 98.1 us -> 90.2 us  [call(): pl.pallas_call(kernel, in_specs=[smem] * len(scalars) + [vmem] * (len(arr...]
    ppermute x15 -> x6, starting transfers between devices: 20.2 us -> 13.2 us  [swap(): lax.ppermute(values, 'blk', [(i, i ^ distance) for i in range(devices)])]
    ppermute x15 -> x6, waiting for transfers between devices: 5.06 us -> 9.41 us  [swap(): lax.ppermute(values, 'blk', [(i, i ^ distance) for i in range(devices)])]
    pallas_call x0 -> x1, Pallas kernels: none -> 1.55 us  [shards(): pl.pallas_call(pack_kernel, in_specs=[smem] + [vmem] * 10, out_specs=vmem...]
  transfers between devices with their start and end apart: 15 -> 6, of which waited for: 5 -> 4; matrix products, arithmetic and copies ran while one was open for 0% -> 0% of each run, Pallas kernels for 40% -> 39%
where the time goes in v3:
time: 117 us
  Pallas kernels  91.7 us (78%)
  starting transfers between devices  13.2 us (11%)
  waiting for transfers between devices  9.41 us (8%)
    pallas_call x3, Pallas kernels, call(): pl.pallas_call(kernel, in_specs=[smem] * len(scalars) + [vmem] * (len(arr...  90.2 us
    ppermute x6, starting transfers between devices, swap(): lax.ppermute(values, 'blk', [(i, i ^ distance) for i in range(devices)])  13.2 us
    ppermute x6, waiting for transfers between devices, swap(): lax.ppermute(values, 'blk', [(i, i ^ distance) for i in range(devices)])  9.41 us
  transfers between devices with their start and end apart: 6, of which 4 were waited for; matrix products, arithmetic and copies ran while one was open for 0% of the time, Pallas kernels for 39%

profile of v3, /device:TPU:0, one launch (start us, length us, event | category | flops | bytes accessed | tf_op | source)
XLA Modules:
  0.0 116.8 jit_solution(1240257417993651049)
XLA Ops:
  0.6 1.6 %pack.1 = f32[1,8,2048]{2,1,0:T(8,128)} custom-call(s32[3]{0:T(128)} %line_platform_ref.3, f32[3,2048]{1,0:T(4,128)} %pos_ref.3, f32[3,2048]{1,0:T(4,128)} %vorticity_ref.1, s32[1,2048]{1,0:T(1,128)} %bitcast.15, f32[3,128]{1,0:T(4,128)} %node_pos_ref.1, f32[3,128]{1,0:T(4,128)} %lever_arm_ref.1, f32[1,128]{1,0:T(1,128)} %bitcast.16, s32[1,128]{1,0:T(1,128)} %bitcast.17, ...), custom_call_target="tpu_custom_call" | custom-call | tf_op jit(solution)/shard_map/pack/pallas_call | solution.py:475
  2.2 0.0 copy-start.9
  2.2 0.5 collective-permute-start
  2.6 1.1 collective-permute-done
  3.8 0.9 pad_maximum_fusion.2
  4.6 2.9 %collective-permute-start.1 = (f32[2,8,2048]{2,1,0:T(8,128)S(1)}, f32[2,8,2048]{2,1,0:T(8,128)S(1)}, u32[]{:S(2)}, u32[]{:S(2)}) collective-permute-start(f32[2,8,2048]{2,1,0:T(8,128)S(1)} %pad_maximum_fusion.2), channel_id=1, source_target_pairs={{0,2},{1,3},{2,0},{3,1},{4,6},{5,7},{6,4},{7,5},{8,10},{9,11},{10,... | collective-permute-start | bytes 393224 | tf_op jit(solution)/shard_map/ppermute | solution.py:496
  7.5 3.8 %collective-permute-done.1 = f32[2,8,2048]{2,1,0:T(8,128)S(1)} collective-permute-done((f32[2,8,2048]{2,1,0:T(8,128)S(1)}, f32[2,8,2048]{2,1,0:T(8,128)S(1)}, u32[]{:S(2)}, u32[]{:S(2)}) %collective-permute-start.1) | collective-permute-done | bytes 131104 | tf_op jit(solution)/shard_map/ppermute | solution.py:496
  11.4 0.0 copy-done.9
  11.4 0.0 copy-start.3
  11.5 1.9 %collective-permute-start.2 = (f32[4,2048]{1,0:T(4,128)S(1)}, f32[4,2048]{1,0:T(4,128)S(1)}, u32[]{:S(2)}, u32[]{:S(2)}) collective-permute-start(f32[4,2048]{1,0:T(4,128)S(1)} %bitcast.12), channel_id=1, source_target_pairs={{0,4},{1,5},{2,6},{3,7},{4,0},{5,1},{6,2},{7,3},{8,12},{9,13},{10,... | collective-permute-start | bytes 98312 | tf_op jit(solution)/shard_map/ppermute | solution.py:496
  13.3 2.1 %collective-permute-done.2 = f32[4,2048]{1,0:T(4,128)S(1)} collective-permute-done((f32[4,2048]{1,0:T(4,128)S(1)}, f32[4,2048]{1,0:T(4,128)S(1)}, u32[]{:S(2)}, u32[]{:S(2)}) %collective-permute-start.2) | collective-permute-done | bytes 32800 | tf_op jit(solution)/shard_map/ppermute | solution.py:496
  15.5 2.9 %collective-permute-start.3 = (f32[8,2048]{1,0:T(8,128)S(1)}, f32[8,2048]{1,0:T(8,128)S(1)}, u32[]{:S(2)}, u32[]{:S(2)}) collective-permute-start(f32[8,2048]{1,0:T(8,128)S(1)} %pad_maximum_fusion.4), channel_id=1, source_target_pairs={{0,8},{1,9},{2,10},{3,11},{4,12},{5,13},{6,14},{7,15},{8,0},{9,1},... | collective-permute-start | bytes 196616 | tf_op jit(solution)/shard_map/ppermute | solution.py:496
  18.3 0.0 copy-start
  18.3 0.0 copy-start.4
  18.3 2.4 %collective-permute-done.3 = f32[8,2048]{1,0:T(8,128)S(1)} collective-permute-done((f32[8,2048]{1,0:T(8,128)S(1)}, f32[8,2048]{1,0:T(8,128)S(1)}, u32[]{:S(2)}, u32[]{:S(2)}) %collective-permute-start.3) | collective-permute-done | bytes 65568 | tf_op jit(solution)/shard_map/ppermute | solution.py:496
  20.7 0.0 copy-start.1
  20.7 0.0 copy-start.5
  20.7 1.9 %collective-permute-start.4 = (f32[4,8,2048]{2,1,0:T(8,128)S(1)}, f32[4,8,2048]{2,1,0:T(8,128)S(1)}, u32[]{:S(2)}, u32[]{:S(2)}) collective-permute-start(f32[4,8,2048]{2,1,0:T(8,128)S(1)} %pad_maximum_fusion.1.base_ref), channel_id=1, source_target_pairs={{0,4},{1,5},{2,6},{3,7},{4,0},{5,1},{6,2},{7,3},{8,12},{9,13},{10,... | collective-permute-start | bytes 786440 | tf_op jit(solution)/shard_map/ppermute | solution.py:496
  22.6 0.0 copy-start.2
  22.6 0.0 copy-start.7
  22.6 0.0 copy-start.8
  22.6 0.0 copy-done.3
  22.6 0.0 copy-done
  22.6 0.0 copy-done.4
  22.6 0.0 copy-done.1
  22.7 0.0 copy-done.5
  22.7 0.6 copy-done.2
  23.3 0.0 copy-done.7
  23.3 0.0 copy-done.8
  23.3 23.0 %pairs.3 = (f32[3,2304]{1,0:T(4,128)S(1)}, f32[16,128]{1,0:T(8,128)S(1)}, f32[3,3,128]{2,1,0:T(4,128)}, f32[9,16,256]{2,1,0:T(8,128)S(1)}) custom-call(s32[1]{0:T(128)} %bitcast.me_ref, f32[16,16]{1,0:T(8,128)S(1)} %slice.7.table_ref, f32[16]{0:T(128)S(1)} %copy-done.8, f32[6]{0:T(128)S(1)} %copy-done.7, s32[3]{0:T(128)S(1)} %copy-done.2, ...), custom_call_target="tpu_custom_call" | custom-call | flops 21390950400 | bytes 262144 | tf_op jit(solution)/shard_map/pairs/pallas_call | solution.py:516
  46.4 0.0 collective-permute-done.4.rest_0_
  46.4 3.3 %collective-permute-start.5 = (f32[8,8,2048]{2,1,0:T(8,128)S(1)}, f32[8,8,2048]{2,1,0:T(8,128)S(1)}, u32[]{:S(2)}, u32[]{:S(2)}) collective-permute-start(f32[8,8,2048]{2,1,0:T(8,128)S(1)} %pad_maximum_fusion), channel_id=1, source_target_pairs={{0,8},{1,9},{2,10},{3,11},{4,12},{5,13},{6,14},{7,15},{8,0},{9,1},... | collective-permute-start | bytes 1572872 | tf_op jit(solution)/shard_map/ppermute | solution.py:496
  49.7 0.0 copy-start.6
  49.7 22.5 %pairs.4.before_ref = f32[9,16,256]{2,1,0:T(8,128)S(1)} custom-call(s32[1]{0:T(128)} %bitcast.me_ref, f32[16,16]{1,0:T(8,128)S(1)} %slice.7.table_ref, f32[16]{0:T(128)S(1)} %copy-done.8, f32[3,2304]{1,0:T(4,128)S(1)} %get-tuple-element.16.target_pos_ref, f32[9,16,256]{2,1,0:T(8,128)S(1)} %get-tuple-element.18.before_ref, ...), custom_call_target="tpu_custom_call" | custom-call | flops 21390950400 | bytes 262144 | tf_op jit(solution)/shard_map/pairs/pallas_call | solution.py:516
  72.2 0.0 collective-permute-done.5.rest_0_
  72.2 0.0 copy-done.6
  72.2 44.6 %pairs.5 = (f32[3,2048]{1,0:T(4,128)}, f32[1,6]{1,0:T(1,128)}, f32[9,16,256]{2,1,0:T(8,128)}) custom-call(s32[1]{0:T(128)} %bitcast.me_ref, f32[16,16]{1,0:T(8,128)S(1)} %slice.7.table_ref, f32[16]{0:T(128)S(1)} %copy-done.8, f32[6,6]{1,0:T(8,128)S(1)} %copy-done.6, f32[3,2304]{1,0:T(4,128)S(1)} %get-tuple-element.16.target_pos_ref, ...), custom_call_target="tpu_custom_call" | custom-call | flops 42781900800 | bytes 524288 | tf_op jit(solution)/shard_map/pairs/pallas_call | solution.py:516
  (7 shorter events, 0.1 us)
Async XLA Ops:
  2.2 9.2 %copy-start.9 = (f32[1,8,2048]{2,1,0:T(8,128)S(1)}, f32[1,8,2048]{2,1,0:T(8,128)}, u32[]{:S(2)}) copy-start(f32[1,8,2048]{2,1,0:T(8,128)} %pack.1) | copy-start | bytes 196612
  2.2 1.6 %collective-permute-start = (f32[1,8,2048]{2,1,0:T(8,128)}, f32[1,8,2048]{2,1,0:T(8,128)S(1)}, u32[]{:S(2)}, u32[]{:S(2)}) collective-permute-start(f32[1,8,2048]{2,1,0:T(8,128)} %pack.1), channel_id=1, source_target_pairs={{0,1},{1,0},{2,3},{3,2},{4,5},{5,4},{6,7},{7,6},{8,9},{9,8},{10,11... | collective-permute-start | bytes 196616 | tf_op jit(solution)/shard_map/ppermute | solution.py:496
  4.6 6.7 %collective-permute-start.1 = (f32[2,8,2048]{2,1,0:T(8,128)S(1)}, f32[2,8,2048]{2,1,0:T(8,128)S(1)}, u32[]{:S(2)}, u32[]{:S(2)}) collective-permute-start(f32[2,8,2048]{2,1,0:T(8,128)S(1)} %pad_maximum_fusion.2), channel_id=1, source_target_pairs={{0,2},{1,3},{2,0},{3,1},{4,6},{5,7},{6,4},{7,5},{8,10},{9,11},{10,... | collective-permute-start | bytes 393224 | tf_op jit(solution)/shard_map/ppermute | solution.py:496
  11.4 11.2 %copy-start.3 = (f32[6,6,1024]{2,1,0:T(8,128)S(1)}, f32[6,6,1024]{2,1,0:T(8,128)}, u32[]{:S(2)}) copy-start(f32[6,6,1024]{2,1,0:T(8,128)} %memory_ref.1) | copy-start | bytes 442372
  11.5 4.0 %collective-permute-start.2 = (f32[4,2048]{1,0:T(4,128)S(1)}, f32[4,2048]{1,0:T(4,128)S(1)}, u32[]{:S(2)}, u32[]{:S(2)}) collective-permute-start(f32[4,2048]{1,0:T(4,128)S(1)} %bitcast.12), channel_id=1, source_target_pairs={{0,4},{1,5},{2,6},{3,7},{4,0},{5,1},{6,2},{7,3},{8,12},{9,13},{10,... | collective-permute-start | bytes 98312 | tf_op jit(solution)/shard_map/ppermute | solution.py:496
  15.5 5.2 %collective-permute-start.3 = (f32[8,2048]{1,0:T(8,128)S(1)}, f32[8,2048]{1,0:T(8,128)S(1)}, u32[]{:S(2)}, u32[]{:S(2)}) collective-permute-start(f32[8,2048]{1,0:T(8,128)S(1)} %pad_maximum_fusion.4), channel_id=1, source_target_pairs={{0,8},{1,9},{2,10},{3,11},{4,12},{5,13},{6,14},{7,15},{8,0},{9,1},... | collective-permute-start | bytes 196616 | tf_op jit(solution)/shard_map/ppermute | solution.py:496
  18.3 4.3 %copy-start = (f32[3,2048]{1,0:T(4,128)S(1)}, f32[3,2048]{1,0:T(4,128)}, u32[]{:S(2)}) copy-start(f32[3,2048]{1,0:T(4,128)} %pos_ref.3) | copy-start | bytes 73732
  18.3 4.3 %copy-start.4 = (f32[1,6,1024]{2,0,1:T(1,128)S(1)}, f32[1,6,1024]{2,0,1:T(1,128)}, u32[]{:S(2)}) copy-start(f32[1,6,1024]{2,0,1:T(1,128)} %param.27) | copy-start | bytes 73732
  20.7 1.9 %copy-start.1 = (f32[3,3,128]{2,1,0:T(4,128)S(1)}, f32[3,3,128]{2,1,0:T(4,128)}, u32[]{:S(2)}) copy-start(f32[3,3,128]{2,1,0:T(4,128)} %offset_ref.3) | copy-start | bytes 13828
  20.7 1.9 %copy-start.5 = (f32[3,3,128]{2,1,0:T(4,128)S(1)}, f32[3,3,128]{2,1,0:T(4,128)}, u32[]{:S(2)}) copy-start(f32[3,3,128]{2,1,0:T(4,128)} %line_velocity_ref.1) | copy-start | bytes 13828
  20.7 25.6 %collective-permute-start.4 = (f32[4,8,2048]{2,1,0:T(8,128)S(1)}, f32[4,8,2048]{2,1,0:T(8,128)S(1)}, u32[]{:S(2)}, u32[]{:S(2)}) collective-permute-start(f32[4,8,2048]{2,1,0:T(8,128)S(1)} %pad_maximum_fusion.1.base_ref), channel_id=1, source_target_pairs={{0,4},{1,5},{2,6},{3,7},{4,0},{5,1},{6,2},{7,3},{8,12},{9,13},{10,... | collective-permute-start | bytes 786440 | tf_op jit(solution)/shard_map/ppermute | solution.py:496
  22.6 0.7 copy-start.2
  22.6 0.7 copy-start.7
  22.6 0.7 copy-start.8
  46.4 25.8 %collective-permute-start.5 = (f32[8,8,2048]{2,1,0:T(8,128)S(1)}, f32[8,8,2048]{2,1,0:T(8,128)S(1)}, u32[]{:S(2)}, u32[]{:S(2)}) collective-permute-start(f32[8,8,2048]{2,1,0:T(8,128)S(1)} %pad_maximum_fusion), channel_id=1, source_target_pairs={{0,8},{1,9},{2,10},{3,11},{4,12},{5,13},{6,14},{7,15},{8,0},{9,1},... | collective-permute-start | bytes 1572872 | tf_op jit(solution)/shard_map/ppermute | solution.py:496
  49.7 22.5 %copy-start.6 = (f32[6,6]{1,0:T(8,128)S(1)}, f32[6,6]{1,0:T(8,128)}, u32[]{:S(2)}) copy-start(f32[6,6]{1,0:T(8,128)} %mass_ref.1) | copy-start | bytes 436
